TPU v7x, 128 devices: a whole 4x4x4 slice. The times are simulated.
128 devices in a mesh: owner: 128 (over y, z, x, core).
Axes of the slice: x: 4, y: 4, z: 4, core: 2. Of those that a mesh axis runs over, the one named last changes fastest.
Arguments:
- coarse: float32 [128, 3, 256, 256], P('owner'), may hold values from 0 to 1.5
- parents: int32 [256], P('owner'), may hold values from 0 to 3, as said below
- new_counts: int32 [128], replicated, may hold values from 1 to 3, as said below
- neighbours: int32 [256, 4], replicated, may hold values from -1 to 255, as said below
- land_cover: int32 [384, 256, 256], P('owner'), may hold values from 0 to 10
- class_diffusivity: float32 [11], replicated, may hold values from 0.05 to 0.25
- class_growth: float32 [11], replicated, may hold values from 0.2 to 1
Outputs:
- fields: float32 [384, 3, 256, 256], P('owner')
Inputs may be any that keep to these rules, and one draw needn't show every extreme that they name: `parents`: within the 2 entries of one old owner the values differ; value p names quadrant p % 4 of the owner's local coarse patch p // 4. `new_counts`: each aligned block of 2 owners holds 4 patches in all; every owner holds at least one. The table is symmetric: if h = neighbours[g, f] is not -1, then neighbours[h, f ^ 1] = g. A neighbour's index differs from g by at most 3; -1 marks the domain's edge.
All inputs are finite; a program needn't handle non-finite values.
Results may differ from a plain program's by a relative error of at most 0.00005.
Values sent between devices are 32-bit elements; how exact they have to be, the bound alone decides.
A program may use at most 128 MiB of HBM per device.

v0:
```python
import functools

import jax
import jax.numpy as jnp
from jax import lax
from jax.experimental import pallas as pl
from jax.experimental.pallas import tpu as pltpu
from jax.sharding import PartitionSpec as P

SIDE = 256
HALF = 128
CLASSES = 11
PAD = 8
WEIGHTS = (0.5, 0.5, 1.0, 1.0 / 6.0)
MESH = pl.DeviceIdType.MESH


def iota(shape, dim):
    return lax.broadcasted_iota(jnp.int32, shape, dim)


def prolong_weights(fine, coarse):
    near = fine >> 1
    second = jnp.clip(near + jnp.where((fine & 1) == 0, -1, 1), 0, HALF - 1)
    heavy = jnp.where(coarse == near, 0.75, 0.0)
    light = jnp.where(coarse == second, 0.25, 0.0)
    return (heavy + light).astype(jnp.bfloat16)


def split(block, axis):
    high = block.astype(jnp.bfloat16)
    low = (block - high.astype(jnp.float32)).astype(jnp.bfloat16)
    return jnp.concatenate([high, low], axis=axis)


def dot(a, b):
    return jnp.dot(a, b, preferred_element_type=jnp.float32)


def dot_t(a, b):
    return lax.dot_general(a, b, (((1,), (1,)), ((), ())), preferred_element_type=jnp.float32)


def look_up(classes, diff_ref, grow_ref):
    diffus = jnp.full(classes.shape, diff_ref[0], jnp.float32)
    growth = jnp.full(classes.shape, grow_ref[0], jnp.float32)
    for number in range(1, CLASSES):
        hit = classes == jnp.asarray(number, classes.dtype)
        diffus = jnp.where(hit, diff_ref[number], diffus)
        growth = jnp.where(hit, grow_ref[number], growth)
    return diffus, growth


def scaled_rates(weight, x0, x1, x2, lap0, lap1, lap2, diffus, growth):
    dw = diffus * weight
    gw = growth * weight
    xw = x0 * weight
    r0 = dw * lap0 + (gw * x0) * (x1 - x0 - x2)
    r1 = (0.5 * dw) * lap1 + (0.4 * weight - x1 * (0.4 * weight + xw))
    r2 = dw * lap2 + (xw - (0.3 * weight) * x2)
    return r0, r1, r2


def combine(x, s2, s3, s4, rate):
    return (s2 + 2.0 * s3 + s4 - x) * (1.0 / 3.0) + rate


def kernel(
    owners,
    parents_ref,
    counts_ref,
    nb_ref,
    diff_ref,
    grow_ref,
    coarse_ref,
    land_ref,
    out_ref,
    quads,
    land,
    x_buf,
    s2_buf,
    s3_buf,
    s4_buf,
    diffus_buf,
    growth_buf,
    result,
    ring,
    across,
    t0,
    t1,
    t2,
    t3,
    strip_diffus,
    strip_growth,
    f0,
    f1,
    f2,
    f3,
    load_sem,
    land_sem,
    face_send,
    face_recv,
    pair_send,
    pair_recv,
):
    me = lax.axis_index("owner")
    parity = me % 2
    partner = me + 1 - 2 * parity
    moving = 1 - parity
    up1, up2 = (me + 1) % owners, (me + 2) % owners
    dn1, dn2 = (me + owners - 1) % owners, (me + owners - 2) % owners
    stages = (x_buf, s2_buf, s3_buf, s4_buf)
    strips = (t0, t1, t2, t3)
    faces = (f0, f1, f2, f3)

    loads = []
    for q in range(4):
        block = coarse_ref.at[0, :, pl.ds((q // 2) * HALF, HALF), pl.ds((q % 2) * HALF, HALF)]
        loads.append(pltpu.make_async_copy(block, quads.at[q], load_sem.at[q]))
    for load in loads:
        load.start()
    land_load = pltpu.make_async_copy(land_ref, land.at[pl.ds(0, 3)], land_sem)
    land_load.start()
    barrier = pltpu.get_barrier_semaphore()
    for other in (up1, dn1, up2, dn2):
        pl.semaphore_signal(barrier, inc=1, device_id=(other,), device_id_type=MESH)

    shape = (SIDE, SIDE)
    columns_up = prolong_weights(iota(shape, 1), iota(shape, 0) & (HALF - 1))
    rows_up = prolong_weights(iota(shape, 0), iota(shape, 1) & (HALF - 1))
    edge = iota((16, SIDE), 0)
    edge = jnp.where(edge < 8, edge, edge + (SIDE - 16))
    edge_up = prolong_weights(edge, iota((16, SIDE), 1) & (HALF - 1))
    edge_pick = jnp.where(iota((16, SIDE), 1) == edge, 1.0, 0.0).astype(jnp.bfloat16)
    for buf in stages:
        for i in range(2):
            for c in range(3):
                for j in range(2):
                    buf[i, c, j, 0:PAD] = jnp.zeros((PAD, HALF), jnp.float32)
                    buf[i, c, j, PAD + SIDE :] = jnp.zeros((PAD, HALF), jnp.float32)

    def send_faces(s, start):
        f = faces[s]
        copies = [
            (f.at[pl.ds(3, 2)], f.at[pl.ds(1, 2)], up1),
            (f.at[pl.ds(3, 2)], f.at[pl.ds(5, 2)], dn1),
            (f.at[4], f.at[0], up2),
            (f.at[3], f.at[7], dn2),
        ]
        made = []
        for n, (src, dst, to) in enumerate(copies):
            made.append(
                pltpu.make_async_remote_copy(
                    src_ref=src,
                    dst_ref=dst,
                    send_sem=face_send.at[s, n],
                    recv_sem=face_recv.at[s, n],
                    device_id=(to,),
                    device_id_type=MESH,
                )
            )
        if start:
            for copy in made:
                copy.start()
        return made

    def put_faces(s, c, block):
        for i in range(2):
            for f in range(4):
                row = 7 * (f % 2)
                faces[s][3 + i, 4 * f + c : 4 * f + c + 1, :] = block[4 * i + f, row : row + 1, :]

    for load in loads:
        load.wait()
    parent = [parents_ref[i] % 4 for i in range(2)]
    edges = []
    for i in range(2):
        for c in range(3):
            block = quads[parent[i], c]
            edges.append(dot_t(edge_up, split(block, 1)))
            edges.append(dot(edge_up, split(block, 0)))
    edges = dot(split(jnp.concatenate(edges, axis=0), 1), columns_up).reshape(2, 3, 4, 8, SIDE)
    for c in range(3):
        block = jnp.concatenate([edges[0, c], edges[1, c]], axis=0)
        t0[c] = block
        put_faces(0, c, block)

    pl.semaphore_wait(barrier, 4)
    sent = send_faces(0, True)
    land_copy = pltpu.make_async_remote_copy(
        src_ref=land_ref.at[2 * (1 - parity)],
        dst_ref=land.at[3],
        send_sem=pair_send.at[0],
        recv_sem=pair_recv.at[0],
        device_id=(partner,),
        device_id_type=MESH,
    )
    land_copy.start()

    for i in range(2):
        for c in range(3):
            half_done = dot(split(quads[parent[i], c], 1), columns_up)
            fine = dot(rows_up, split(half_done, 0))
            for j in range(2):
                x_buf[i, c, j, PAD : PAD + SIDE] = fine[:, j * HALF : (j + 1) * HALF]

    land_load.wait()
    land_copy.wait_recv()
    count = counts_ref[me]
    slots = []
    for i in range(2):
        even_slot = jnp.where(i >= count, 3, i)
        odd_slot = jnp.where(i - 2 + count < 0, 3, i - 2 + count)
        slots.append(jnp.where(parity == 0, even_slot, odd_slot))
    for i in range(2):
        picked = dot_t(edge_pick, land[slots[i]].astype(jnp.float32).astype(jnp.bfloat16))
        across_d, across_g = look_up(picked, diff_ref, grow_ref)
        ends = jnp.concatenate(
            [land[slots[i], 0:8, :], land[slots[i], SIDE - 8 : SIDE, :]], axis=0
        )
        along_d, along_g = look_up(ends, diff_ref, grow_ref)
        for n in range(2):
            rows = slice(8 * n, 8 * n + 8)
            strip_diffus[4 * i + n] = across_d[rows]
            strip_growth[4 * i + n] = across_g[rows]
            strip_diffus[4 * i + 2 + n] = along_d[rows]
            strip_growth[4 * i + 2 + n] = along_g[rows]

        def fill(step, carry, i=i):
            r = pl.multiple_of(step * 8, 8)
            for j in range(2):
                d, g = look_up(
                    land[slots[i], pl.ds(r, 8), j * HALF : (j + 1) * HALF], diff_ref, grow_ref
                )
                diffus_buf[i, j, pl.ds(r, 8), :] = d
                growth_buf[i, j, pl.ds(r, 8), :] = g
            return carry

        lax.fori_loop(0, SIDE // 8, fill, 0)

    peers = []
    for i in range(2):
        for f in range(4):
            value = nb_ref[2 * me + i, f]
            peers.append((value >= 0, jnp.clip(value - (2 * me - 3), 0, 7)))

    strip = (8, 8, SIDE)
    sub = iota(strip, 1)
    lane = iota(strip, 2)
    sub_half = iota((8, 8, HALF), 1)
    lane_half = iota((8, 8, HALF), 2)

    def strip_laplacian(s, c):
        now = strips[s][c]
        f_ref = faces[s]
        ghosts = []
        for i in range(2):
            for f in range(4):
                has, where = peers[4 * i + f]
                theirs = 4 * (f ^ 1) + c
                ours = 4 * f + c
                row = jnp.where(
                    has, f_ref[where, theirs : theirs + 1, :], f_ref[3 + i, ours : ours + 1, :]
                )
                ghosts.append(jnp.broadcast_to(row, (8, SIDE)))
        ghost = jnp.stack(ghosts, axis=0)
        low = jnp.sum(
            jnp.where(lane_half == sub_half, ghost[:, :, :HALF], 0.0), axis=2, keepdims=True
        )
        high = jnp.sum(
            jnp.where(lane_half == sub_half + (HALF - 8), ghost[:, :, HALF:], 0.0),
            axis=2,
            keepdims=True,
        )
        ends = []
        for e in range(2):
            columns = []
            for i in range(2):
                for f in range(4):
                    source = (low, high)[f % 2]
                    face = 4 * i + (2 if f < 2 else 0) + e
                    columns.append(source[face])
            ends.append(jnp.stack(columns, axis=0))
        above = jnp.where(sub == 0, ghost, pltpu.roll(now, 1, 1))
        below = jnp.where(sub == 7, ghost, pltpu.roll(now, 7, 1))
        left = jnp.where(lane == 0, ends[0], pltpu.roll(now, 1, 2))
        right = jnp.where(lane == SIDE - 1, ends[1], pltpu.roll(now, SIDE - 1, 2))
        return now, (left + right) + (below + above) - 4.0 * now

    def strip_stage(s):
        values = [strip_laplacian(s, c) for c in range(3)]
        rates = scaled_rates(
            WEIGHTS[s],
            *[v[0] for v in values],
            *[v[1] for v in values],
            strip_diffus[...],
            strip_growth[...],
        )
        for c in range(3):
            if s < 3:
                block = t0[c] + rates[c]
                strips[s + 1][c] = block
                put_faces(s + 1, c, block)
            else:
                block = combine(t0[c], t1[c], t2[c], t3[c], rates[c])
                for i in range(2):
                    ring[i, c] = block[4 * i : 4 * i + 4]

    first_lane = iota((8, HALF), 1) == 0
    last_lane = iota((8, HALF), 1) == HALF - 1

    def bulk_stage(i, s):
        src = stages[s]

        def step_rows(step, carry):
            r = pl.multiple_of(step * 8, 8)
            at = PAD + r
            now = [[None, None] for _ in range(3)]
            lap = [[None, None] for _ in range(3)]
            for c in range(3):
                a = src[i, c, 0, pl.ds(at, 8), :]
                b = src[i, c, 1, pl.ds(at, 8), :]
                now[c] = [a, b]
                a_right, b_right = pltpu.roll(a, 1, 1), pltpu.roll(b, 1, 1)
                a_left, b_left = pltpu.roll(a, HALF - 1, 1), pltpu.roll(b, HALF - 1, 1)
                sides = [
                    a_right + jnp.where(last_lane, b_left, a_left),
                    jnp.where(first_lane, a_right, b_right) + b_left,
                ]
                for j in range(2):
                    above = src[i, c, j, pl.ds(at - 1, 8), :]
                    below = src[i, c, j, pl.ds(at + 1, 8), :]
                    lap[c][j] = sides[j] + (below + above) - 4.0 * now[c][j]
            for j in range(2):
                rates = scaled_rates(
                    WEIGHTS[s],
                    *[now[c][j] for c in range(3)],
                    *[lap[c][j] for c in range(3)],
                    diffus_buf[i, j, pl.ds(r, 8), :],
                    growth_buf[i, j, pl.ds(r, 8), :],
                )
                for c in range(3):
                    base = now[c][j] if s == 0 else x_buf[i, c, j, pl.ds(at, 8), :]
                    if s < 3:
                        stages[s + 1][i, c, j, pl.ds(at, 8), :] = base + rates[c]
                    else:
                        result[i, c, j, pl.ds(r, 8), :] = combine(
                            base,
                            s2_buf[i, c, j, pl.ds(at, 8), :],
                            s3_buf[i, c, j, pl.ds(at, 8), :],
                            now[c][j],
                            rates[c],
                        )
            return carry

        lax.fori_loop(0, SIDE // 8, step_rows, 0, unroll=2)

    result_copy = pltpu.make_async_remote_copy(
        src_ref=result.at[moving],
        dst_ref=result.at[2],
        send_sem=pair_send.at[1],
        recv_sem=pair_recv.at[1],
        device_id=(partner,),
        device_id_type=MESH,
    )
    ring_copy = pltpu.make_async_remote_copy(
        src_ref=ring.at[moving],
        dst_ref=ring.at[2],
        send_sem=pair_send.at[2],
        recv_sem=pair_recv.at[2],
        device_id=(partner,),
        device_id_type=MESH,
    )
    gaps = (((moving, 0), (moving, 1), (moving, 2)), ((moving, 3), (parity, 0), (parity, 1)), ((parity, 2), (parity, 3)))
    for s in range(4):
        for copy in sent[4 * s : 4 * s + 4]:
            copy.wait_recv()
        strip_stage(s)
        if s < 3:
            sent = sent + send_faces(s + 1, True)
            for i, stage in gaps[s]:
                bulk_stage(i, stage)
                if s == 1 and stage == 3:
                    result_copy.start()
    ring_copy.start()

    def turn(e):
        for c in range(3):
            block = jnp.concatenate(
                [ring[e, c, 0], jnp.zeros((HALF - 16, SIDE), jnp.float32), ring[e, c, 1]], axis=0
            )
            across[e, c, 0:HALF] = block[:, :HALF].T
            across[e, c, HALF:SIDE] = block[:, HALF:].T

    turn(0)
    turn(1)
    result_copy.wait_recv()
    ring_copy.wait_recv()
    turn(2)

    low_lanes = iota((8, HALF), 1) < 4
    high_lanes = iota((8, HALF), 1) >= HALF - 4
    sub_rows = iota((8, SIDE), 0)
    sources = []
    for s in range(3):
        from_even = s
        from_odd = (5 - count + s) % 3
        sources.append((jnp.where(parity == 0, from_even, from_odd), s < count))

    def place(step, carry):
        r = pl.multiple_of(step * 8, 8)
        for s in range(3):
            e, held = sources[s]
            for c in range(3):
                side = across[e, c, pl.ds(r, 8), :]
                left = jnp.where(low_lanes, side, result[e, c, 0, pl.ds(r, 8), :])
                right = jnp.where(high_lanes, side, result[e, c, 1, pl.ds(r, 8), :])
                out_ref[s, c, pl.ds(r, 8), 0:HALF] = jnp.where(held, left, 0.0)
                out_ref[s, c, pl.ds(r, 8), HALF:SIDE] = jnp.where(held, right, 0.0)
        return carry

    lax.fori_loop(0, SIDE // 8, place, 0)
    for s in range(3):
        e, held = sources[s]
        for c in range(3):
            for n, rows in ((0, slice(0, 8)), (1, slice(SIDE - 8, SIDE))):
                inside = sub_rows < 4 if n == 0 else sub_rows >= 4
                merged = jnp.where(inside, ring[e, c, 2 + n], out_ref[s, c, rows, :])
                out_ref[s, c, rows, :] = jnp.where(held, merged, 0.0)

    for copy in sent:
        copy.wait_send()
    land_copy.wait_send()
    result_copy.wait_send()
    ring_copy.wait_send()


def body(coarse, parents, new_counts, neighbours, land_cover, class_diffusivity, class_growth):
    owners = lax.axis_size("owner")
    f32 = jnp.float32
    smem = pl.BlockSpec(memory_space=pltpu.SMEM)
    hbm = pl.BlockSpec(memory_space=pl.ANY)
    stage_buf = pltpu.VMEM((2, 3, 2, SIDE + 2 * PAD, HALF), f32)
    strip_buf = pltpu.VMEM((3, 8, 8, SIDE), f32)
    face_buf = pltpu.VMEM((8, 16, SIDE), f32)
    return pl.pallas_call(
        functools.partial(kernel, owners),
        out_shape=jax.ShapeDtypeStruct((3, 3, SIDE, SIDE), f32),
        in_specs=[smem] * 5 + [hbm] * 2,
        out_specs=pl.BlockSpec(memory_space=pltpu.VMEM),
        scratch_shapes=[
            pltpu.VMEM((4, 3, HALF, HALF), f32),
            pltpu.VMEM((4, SIDE, SIDE), jnp.int32),
            stage_buf,
            stage_buf,
            stage_buf,
            stage_buf,
            pltpu.VMEM((2, 2, SIDE, HALF), f32),
            pltpu.VMEM((2, 2, SIDE, HALF), f32),
            pltpu.VMEM((3, 3, 2, SIDE, HALF), f32),
            pltpu.VMEM((3, 3, 4, 8, SIDE), f32),
            pltpu.VMEM((3, 3, SIDE, HALF), f32),
            strip_buf,
            strip_buf,
            strip_buf,
            strip_buf,
            pltpu.VMEM((8, 8, SIDE), f32),
            pltpu.VMEM((8, 8, SIDE), f32),
            face_buf,
            face_buf,
            face_buf,
            face_buf,
            pltpu.SemaphoreType.DMA((4,)),
            pltpu.SemaphoreType.DMA,
            pltpu.SemaphoreType.DMA((4, 4)),
            pltpu.SemaphoreType.DMA((4, 4)),
            pltpu.SemaphoreType.DMA((3,)),
            pltpu.SemaphoreType.DMA((3,)),
        ],
        compiler_params=pltpu.CompilerParams(
            collective_id=0, has_side_effects=True, vmem_limit_bytes=40 * 1024 * 1024
        ),
        name="regrid_step",
    )(parents, new_counts, neighbours, class_diffusivity, class_growth, coarse, land_cover)


def solution(mesh):
    return jax.shard_map(
        body,
        mesh=mesh,
        in_specs=(
            P("owner", None, None, None),
            P("owner"),
            P(),
            P(),
            P("owner", None, None),
            P(),
            P(),
        ),
        out_specs=P("owner", None, None, None),
        check_vma=False,
    )
```

profile of v0, /device:TPU:1, one launch (start us, length us, event | category | flops | bytes accessed | tf_op | source)
XLA Modules:
  0.0 46.2 jit_solution(11405521887283100412)
XLA Ops:
  0.0 0.8 %copy.8.nb_ref = s32[256,4]{1,0:T(8,128)S(1)} copy(s32[256,4]{0,1:T(4,128)} %param.10) | data formatting | bytes 8192 | tf_op args[3]
  0.8 0.0 copy-start
  0.8 1.1 %copy-done = f32[1,3,256,256]{3,2,1,0:T(8,128)S(1)} copy-done((f32[1,3,256,256]{3,2,1,0:T(8,128)S(1)}, f32[1,3,256,256]{3,2,1,0:T(8,128)}, u32[]{:S(2)}) %copy-start) | copy-done | bytes 786456
  2.0 0.0 copy-start.1
  2.0 1.1 %copy-done.1 = s32[3,256,256]{2,1,0:T(8,128)S(1)} copy-done((s32[3,256,256]{2,1,0:T(8,128)S(1)}, s32[3,256,256]{2,1,0:T(8,128)}, u32[]{:S(2)}) %copy-start.1) | copy-done | bytes 786456
  3.1 0.0 copy-start.2
  3.1 0.7 %copy-done.2 = s32[2]{0:T(128)S(1)} copy-done((s32[2]{0:T(128)S(1)}, s32[2]{0:T(128)}, u32[]{:S(2)}) %copy-start.2) | copy-done | bytes 32
  3.8 0.0 copy-start.3
  3.8 0.7 %copy-done.3 = s32[128]{0:T(128)S(1)} copy-done((s32[128]{0:T(128)S(1)}, s32[128]{0:T(128)}, u32[]{:S(2)}) %copy-start.3) | copy-done | bytes 536
  4.4 0.0 copy-start.4
  4.4 0.7 %copy-done.4 = f32[11]{0:T(128)S(1)} copy-done((f32[11]{0:T(128)S(1)}, f32[11]{0:T(128)}, u32[]{:S(2)}) %copy-start.4) | copy-done | bytes 68
  5.1 0.0 copy-start.5
  5.1 0.7 %copy-done.5 = f32[11]{0:T(128)S(1)} copy-done((f32[11]{0:T(128)S(1)}, f32[11]{0:T(128)}, u32[]{:S(2)}) %copy-start.5) | copy-done | bytes 68
  5.7 39.1 %regrid_step.1 = f32[3,3,256,256]{3,2,1,0:T(8,128)S(1)} custom-call(s32[2]{0:T(128)S(1)} %copy-done.2, s32[128]{0:T(128)S(1)} %copy-done.3, s32[256,4]{1,0:T(8,128)S(1)} %copy.8.nb_ref, f32[11]{0:T(128)S(1)} %copy-done.4, f32[11]{0:T(128)S(1)} %copy-done.5, f32[1,3,256,256]{3,2,1,0:T(8,128)S(1)} %copy-done, s32[3,256,256]{2,1,0:T(8,128)S(1)} %copy-done.1), custom_call_target="tpu_custom_call" | custom-call | tf_op jit(solution)/shard_map/regrid_step/pallas_call | solution.py:446
  44.8 1.4 %copy.10 = f32[3,3,256,256]{3,2,1,0:T(8,128)} copy(f32[3,3,256,256]{3,2,1,0:T(8,128)S(1)} %regrid_step.1) | data formatting | bytes 4718592
Async XLA Ops:
  0.8 1.1 %copy-start = (f32[1,3,256,256]{3,2,1,0:T(8,128)S(1)}, f32[1,3,256,256]{3,2,1,0:T(8,128)}, u32[]{:S(2)}) copy-start(f32[1,3,256,256]{3,2,1,0:T(8,128)} %coarse_ref.1) | copy-start | bytes 2359300
  2.0 1.1 %copy-start.1 = (s32[3,256,256]{2,1,0:T(8,128)S(1)}, s32[3,256,256]{2,1,0:T(8,128)}, u32[]{:S(2)}) copy-start(s32[3,256,256]{2,1,0:T(8,128)} %land_ref.1) | copy-start | bytes 2359300
  3.1 0.7 %copy-start.2 = (s32[2]{0:T(128)S(1)}, s32[2]{0:T(128)}, u32[]{:S(2)}) copy-start(s32[2]{0:T(128)} %parents_ref.1) | copy-start | bytes 28
  3.8 0.7 %copy-start.3 = (s32[128]{0:T(128)S(1)}, s32[128]{0:T(128)}, u32[]{:S(2)}) copy-start(s32[128]{0:T(128)} %counts_ref.1) | copy-start | bytes 1540
  4.4 0.7 %copy-start.4 = (f32[11]{0:T(128)S(1)}, f32[11]{0:T(128)}, u32[]{:S(2)}) copy-start(f32[11]{0:T(128)} %diff_ref.1) | copy-start | bytes 136
  5.1 0.7 %copy-start.5 = (f32[11]{0:T(128)S(1)}, f32[11]{0:T(128)}, u32[]{:S(2)}) copy-start(f32[11]{0:T(128)} %grow_ref.1) | copy-start | bytes 136
where the time goes:
time: 46.5 us; the launch traced here: 46.2 us
  Pallas kernels  39.1 us (84%)
  local copies, waits for them, and re-layouts  7.1 us (15%)
    pallas_call x1, Pallas kernels, body(): pl.pallas_call(functools.partial(kernel, owners), out_shape=jax.ShapeDtyp...  39.1 us
    unnamed x14, local copies, waits for them, and re-layouts  7.1 us

commit v1 on v0

--- a/solution.py
+++ b/solution.py
@@ -17,6 +17,10 @@
 
 def iota(shape, dim):
     return lax.broadcasted_iota(jnp.int32, shape, dim)
+
+
+def phased(index):
+    return 2 * (index & (HALF - 1)) + (index >> 7)
 
 
 def prolong_weights(fine, coarse):
@@ -67,14 +71,19 @@
 
 def kernel(
     owners,
+    parents_hbm,
+    counts_hbm,
+    nb_hbm,
+    diff_hbm,
+    grow_hbm,
+    coarse_ref,
+    land_ref,
+    out_ref,
     parents_ref,
     counts_ref,
     nb_ref,
     diff_ref,
     grow_ref,
-    coarse_ref,
-    land_ref,
-    out_ref,
     quads,
     land,
     x_buf,
@@ -97,6 +106,7 @@
     f2,
     f3,
     load_sem,
+    small_sem,
     land_sem,
     face_send,
     face_recv,
@@ -119,6 +129,17 @@
         loads.append(pltpu.make_async_copy(block, quads.at[q], load_sem.at[q]))
     for load in loads:
         load.start()
+    small = []
+    pairs = (
+        (parents_hbm, parents_ref),
+        (counts_hbm, counts_ref),
+        (nb_hbm, nb_ref),
+        (diff_hbm, diff_ref),
+        (grow_hbm, grow_ref),
+    )
+    for n, (src, dst) in enumerate(pairs):
+        small.append(pltpu.make_async_copy(src, dst, small_sem.at[n]))
+        small[n].start()
     land_load = pltpu.make_async_copy(land_ref, land.at[pl.ds(0, 3)], land_sem)
     land_load.start()
     barrier = pltpu.get_barrier_semaphore()
@@ -127,7 +148,10 @@
 
     shape = (SIDE, SIDE)
     columns_up = prolong_weights(iota(shape, 1), iota(shape, 0) & (HALF - 1))
-    rows_up = prolong_weights(iota(shape, 0), iota(shape, 1) & (HALF - 1))
+    phases_across = prolong_weights(phased(iota(shape, 1)), iota(shape, 0) & (HALF - 1))
+    phases_along = prolong_weights(phased(iota(shape, 0)), iota(shape, 1) & (HALF - 1))
+    weave = jnp.where(phased(iota(shape, 0)) == iota(shape, 1), 1.0, 0.0).astype(jnp.bfloat16)
+    unweave = jnp.where(phased(iota(shape, 1)) == iota(shape, 0), 1.0, 0.0).astype(jnp.bfloat16)
     edge = iota((16, SIDE), 0)
     edge = jnp.where(edge < 8, edge, edge + (SIDE - 16))
     edge_up = prolong_weights(edge, iota((16, SIDE), 1) & (HALF - 1))
@@ -135,9 +159,10 @@
     for buf in stages:
         for i in range(2):
             for c in range(3):
-                for j in range(2):
-                    buf[i, c, j, 0:PAD] = jnp.zeros((PAD, HALF), jnp.float32)
-                    buf[i, c, j, PAD + SIDE :] = jnp.zeros((PAD, HALF), jnp.float32)
+                for y in range(2):
+                    for x in range(2):
+                        buf[i, c, y, x, 0:PAD] = jnp.zeros((PAD, HALF), jnp.float32)
+                        buf[i, c, y, x, PAD + HALF :] = jnp.zeros((PAD, HALF), jnp.float32)
 
     def send_faces(s, start):
         f = faces[s]
@@ -170,7 +195,7 @@
                 row = 7 * (f % 2)
                 faces[s][3 + i, 4 * f + c : 4 * f + c + 1, :] = block[4 * i + f, row : row + 1, :]
 
-    for load in loads:
+    for load in loads + small:
         load.wait()
     parent = [parents_ref[i] % 4 for i in range(2)]
     edges = []
@@ -199,10 +224,13 @@
 
     for i in range(2):
         for c in range(3):
-            half_done = dot(split(quads[parent[i], c], 1), columns_up)
-            fine = dot(rows_up, split(half_done, 0))
-            for j in range(2):
-                x_buf[i, c, j, PAD : PAD + SIDE] = fine[:, j * HALF : (j + 1) * HALF]
+            half_done = dot(split(quads[parent[i], c], 1), phases_across)
+            fine = dot(phases_along, split(half_done, 0))
+            for y in range(2):
+                for x in range(2):
+                    x_buf[i, c, y, x, PAD : PAD + HALF] = fine[
+                        y * HALF : (y + 1) * HALF, x * HALF : (x + 1) * HALF
+                    ]
 
     land_load.wait()
     land_copy.wait_recv()
@@ -213,7 +241,8 @@
         odd_slot = jnp.where(i - 2 + count < 0, 3, i - 2 + count)
         slots.append(jnp.where(parity == 0, even_slot, odd_slot))
     for i in range(2):
-        picked = dot_t(edge_pick, land[slots[i]].astype(jnp.float32).astype(jnp.bfloat16))
+        classes = land[slots[i]].astype(jnp.float32).astype(jnp.bfloat16)
+        picked = dot_t(edge_pick, classes)
         across_d, across_g = look_up(picked, diff_ref, grow_ref)
         ends = jnp.concatenate(
             [land[slots[i], 0:8, :], land[slots[i], SIDE - 8 : SIDE, :]], axis=0
@@ -226,22 +255,19 @@
             strip_diffus[4 * i + 2 + n] = along_d[rows]
             strip_growth[4 * i + 2 + n] = along_g[rows]
 
-        def fill(step, carry, i=i):
-            r = pl.multiple_of(step * 8, 8)
-            for j in range(2):
-                d, g = look_up(
-                    land[slots[i], pl.ds(r, 8), j * HALF : (j + 1) * HALF], diff_ref, grow_ref
-                )
-                diffus_buf[i, j, pl.ds(r, 8), :] = d
-                growth_buf[i, j, pl.ds(r, 8), :] = g
-            return carry
-
-        lax.fori_loop(0, SIDE // 8, fill, 0)
+        classes = dot(classes, unweave).astype(jnp.bfloat16)
+        for n in range(8):
+            rows = slice(32 * n, 32 * n + 32)
+            d, g = look_up(dot(weave[rows], classes), diff_ref, grow_ref)
+            y, m = n // 4, 32 * (n % 4)
+            for x in range(2):
+                diffus_buf[i, y, x, m : m + 32] = d[:, x * HALF : (x + 1) * HALF]
+                growth_buf[i, y, x, m : m + 32] = g[:, x * HALF : (x + 1) * HALF]
 
     peers = []
     for i in range(2):
         for f in range(4):
-            value = nb_ref[2 * me + i, f]
+            value = nb_ref[f, 2 * me + i]
             peers.append((value >= 0, jnp.clip(value - (2 * me - 3), 0, 7)))
 
     strip = (8, 8, SIDE)
@@ -306,54 +332,61 @@
                 for i in range(2):
                     ring[i, c] = block[4 * i : 4 * i + 4]
 
-    first_lane = iota((8, HALF), 1) == 0
-    last_lane = iota((8, HALF), 1) == HALF - 1
-
     def bulk_stage(i, s):
         src = stages[s]
+        dst = stages[(s + 1) % 4] if s < 3 else s2_buf
 
         def step_rows(step, carry):
             r = pl.multiple_of(step * 8, 8)
             at = PAD + r
-            now = [[None, None] for _ in range(3)]
-            lap = [[None, None] for _ in range(3)]
+            here = pl.ds(at, 8)
+            now = [[src[i, c, n // 2, n % 2, here, :] for n in range(4)] for c in range(3)]
+            lap = [[None] * 4 for _ in range(3)]
             for c in range(3):
-                a = src[i, c, 0, pl.ds(at, 8), :]
-                b = src[i, c, 1, pl.ds(at, 8), :]
-                now[c] = [a, b]
-                a_right, b_right = pltpu.roll(a, 1, 1), pltpu.roll(b, 1, 1)
-                a_left, b_left = pltpu.roll(a, HALF - 1, 1), pltpu.roll(b, HALF - 1, 1)
-                sides = [
-                    a_right + jnp.where(last_lane, b_left, a_left),
-                    jnp.where(first_lane, a_right, b_right) + b_left,
-                ]
-                for j in range(2):
-                    above = src[i, c, j, pl.ds(at - 1, 8), :]
-                    below = src[i, c, j, pl.ds(at + 1, 8), :]
-                    lap[c][j] = sides[j] + (below + above) - 4.0 * now[c][j]
-            for j in range(2):
+                for n in range(4):
+                    y, x = n // 2, n % 2
+                    beside = now[c][2 * y + 1 - x]
+                    beyond = pltpu.roll(beside, HALF - 1 if x else 1, 1)
+                    upright = now[c][2 * (1 - y) + x]
+                    further = src[i, c, 1 - y, x, pl.ds(at + 2 * y - 1, 8), :]
+                    lap[c][n] = (beside + beyond) + (upright + further) - 4.0 * now[c][n]
+            for n in range(4):
+                y, x = n // 2, n % 2
                 rates = scaled_rates(
                     WEIGHTS[s],
-                    *[now[c][j] for c in range(3)],
-                    *[lap[c][j] for c in range(3)],
-                    diffus_buf[i, j, pl.ds(r, 8), :],
-                    growth_buf[i, j, pl.ds(r, 8), :],
+                    *[now[c][n] for c in range(3)],
+                    *[lap[c][n] for c in range(3)],
+                    diffus_buf[i, y, x, pl.ds(r, 8), :],
+                    growth_buf[i, y, x, pl.ds(r, 8), :],
                 )
                 for c in range(3):
-                    base = now[c][j] if s == 0 else x_buf[i, c, j, pl.ds(at, 8), :]
+                    base = now[c][n] if s == 0 else x_buf[i, c, y, x, here, :]
                     if s < 3:
-                        stages[s + 1][i, c, j, pl.ds(at, 8), :] = base + rates[c]
+                        value = base + rates[c]
                     else:
-                        result[i, c, j, pl.ds(r, 8), :] = combine(
+                        value = combine(
                             base,
-                            s2_buf[i, c, j, pl.ds(at, 8), :],
-                            s3_buf[i, c, j, pl.ds(at, 8), :],
-                            now[c][j],
+                            s2_buf[i, c, y, x, here, :],
+                            s3_buf[i, c, y, x, here, :],
+                            now[c][n],
                             rates[c],
                         )
+                    dst[i, c, y, x, here, :] = value
             return carry
 
-        lax.fori_loop(0, SIDE // 8, step_rows, 0, unroll=2)
+        lax.fori_loop(0, HALF // 8, step_rows, 0, unroll=4)
+
+    def bulk_weave(i):
+        for c in range(3):
+            for y in range(2):
+                both = jnp.concatenate(
+                    [s2_buf[i, c, y, x, PAD : PAD + HALF, :] for x in range(2)], axis=1
+                )
+                high = both.astype(jnp.bfloat16)
+                low = (both - high.astype(jnp.float32)).astype(jnp.bfloat16)
+                woven = dot(high, weave) + dot(low, weave)
+                for j in range(2):
+                    result[i, c, j, pl.ds(y, HALF, stride=2), :] = woven[:, j * HALF : (j + 1) * HALF]
 
     result_copy = pltpu.make_async_remote_copy(
         src_ref=result.at[moving],
@@ -371,7 +404,11 @@
         device_id=(partner,),
         device_id_type=MESH,
     )
-    gaps = (((moving, 0), (moving, 1), (moving, 2)), ((moving, 3), (parity, 0), (parity, 1)), ((parity, 2), (parity, 3)))
+    gaps = (
+        ((moving, 0), (moving, 1), (moving, 2)),
+        ((moving, 3), (moving, 4), (parity, 0)),
+        ((parity, 1), (parity, 2), (parity, 3), (parity, 4)),
+    )
     for s in range(4):
         for copy in sent[4 * s : 4 * s + 4]:
             copy.wait_recv()
@@ -379,8 +416,11 @@
         if s < 3:
             sent = sent + send_faces(s + 1, True)
             for i, stage in gaps[s]:
-                bulk_stage(i, stage)
-                if s == 1 and stage == 3:
+                if stage < 4:
+                    bulk_stage(i, stage)
+                else:
+                    bulk_weave(i)
+                if s == 1 and stage == 4:
                     result_copy.start()
     ring_copy.start()
 
@@ -438,25 +478,29 @@
 def body(coarse, parents, new_counts, neighbours, land_cover, class_diffusivity, class_growth):
     owners = lax.axis_size("owner")
     f32 = jnp.float32
-    smem = pl.BlockSpec(memory_space=pltpu.SMEM)
-    hbm = pl.BlockSpec(memory_space=pl.ANY)
-    stage_buf = pltpu.VMEM((2, 3, 2, SIDE + 2 * PAD, HALF), f32)
+    hbm = pl.BlockSpec(memory_space=pltpu.HBM)
+    stage_buf = pltpu.VMEM((2, 3, 2, 2, HALF + 2 * PAD, HALF), f32)
     strip_buf = pltpu.VMEM((3, 8, 8, SIDE), f32)
     face_buf = pltpu.VMEM((8, 16, SIDE), f32)
     return pl.pallas_call(
         functools.partial(kernel, owners),
         out_shape=jax.ShapeDtypeStruct((3, 3, SIDE, SIDE), f32),
-        in_specs=[smem] * 5 + [hbm] * 2,
+        in_specs=[hbm] * 7,
         out_specs=pl.BlockSpec(memory_space=pltpu.VMEM),
         scratch_shapes=[
+            pltpu.SMEM((2,), jnp.int32),
+            pltpu.SMEM((owners,), jnp.int32),
+            pltpu.SMEM((4, 2 * owners), jnp.int32),
+            pltpu.SMEM((CLASSES,), f32),
+            pltpu.SMEM((CLASSES,), f32),
             pltpu.VMEM((4, 3, HALF, HALF), f32),
             pltpu.VMEM((4, SIDE, SIDE), jnp.int32),
             stage_buf,
             stage_buf,
             stage_buf,
             stage_buf,
-            pltpu.VMEM((2, 2, SIDE, HALF), f32),
-            pltpu.VMEM((2, 2, SIDE, HALF), f32),
+            pltpu.VMEM((2, 2, 2, HALF, HALF), f32),
+            pltpu.VMEM((2, 2, 2, HALF, HALF), f32),
             pltpu.VMEM((3, 3, 2, SIDE, HALF), f32),
             pltpu.VMEM((3, 3, 4, 8, SIDE), f32),
             pltpu.VMEM((3, 3, SIDE, HALF), f32),
@@ -471,6 +515,7 @@
             face_buf,
             face_buf,
             pltpu.SemaphoreType.DMA((4,)),
+            pltpu.SemaphoreType.DMA((5,)),
             pltpu.SemaphoreType.DMA,
             pltpu.SemaphoreType.DMA((4, 4)),
             pltpu.SemaphoreType.DMA((4, 4)),
@@ -478,10 +523,10 @@
             pltpu.SemaphoreType.DMA((3,)),
         ],
         compiler_params=pltpu.CompilerParams(
-            collective_id=0, has_side_effects=True, vmem_limit_bytes=40 * 1024 * 1024
+            collective_id=0, has_side_effects=True, vmem_limit_bytes=62 * 1024 * 1024
         ),
         name="regrid_step",
-    )(parents, new_counts, neighbours, class_diffusivity, class_growth, coarse, land_cover)
+    )(parents, new_counts, neighbours.T, class_diffusivity, class_growth, coarse, land_cover)
 
 
 def solution(mesh):

time: 46.5 us -> 41 us (0.88)
  local copies, waits for them, and re-layouts: 7.1 us -> 3.22 us
  Pallas kernels: 39.1 us -> 37.6 us
    unnamed x14 -> x1, local copies, waits for them, and re-layouts: 7.1 us -> 3.22 us
    pallas_call x1, Pallas kernels: 39.1 us -> 37.6 us  [body(): pl.pallas_call(functools.partial(kernel, owners), out_shape=jax.ShapeDtyp...]
where the time goes in v1:
time: 41 us; the launch traced here: 40.9 us
  Pallas kernels  37.6 us (92%)
  local copies, waits for them, and re-layouts  3.22 us (8%)
    pallas_call x1, Pallas kernels, body(): pl.pallas_call(functools.partial(kernel, owners), out_shape=jax.ShapeDtyp...  37.6 us
    unnamed x1, local copies, waits for them, and re-layouts  3.22 us

profile of v1, /device:TPU:1, one launch (start us, length us, event | category | flops | bytes accessed | tf_op | source)
XLA Modules:
  0.0 40.9 jit_solution(7372198355325301270)
XLA Ops:
  0.0 37.6 %regrid_step.1 = f32[3,3,256,256]{3,2,1,0:T(8,128)} custom-call(s32[2]{0:T(128)} %parents_hbm.1, s32[128]{0:T(128)} %counts_hbm.1, s32[4,256]{1,0:T(4,128)} %bitcast.1, f32[11]{0:T(128)} %diff_hbm.1, f32[11]{0:T(128)} %grow_hbm.1, f32[1,3,256,256]{3,2,1,0:T(8,128)} %coarse_ref.1, s32[3,256,256]{2,1,0:T(8,128)} %land_ref.1), custom_call_target="tpu_custom_call" | custom-call | tf_op jit(solution)/shard_map/regrid_step/pallas_call | solution.py:485
  37.7 3.2 %copy.9 = f32[3,3,256,256]{3,2,1,0:T(8,128)} copy(f32[3,3,256,256]{3,2,1,0:T(8,128)} %regrid_step.1) | data formatting | bytes 4718592

commit v2 on v1

--- a/solution.py
+++ b/solution.py
@@ -78,7 +78,8 @@
     grow_hbm,
     coarse_ref,
     land_ref,
-    out_ref,
+    result_out,
+    ring_out,
     parents_ref,
     counts_ref,
     nb_ref,
@@ -94,7 +95,6 @@
     growth_buf,
     result,
     ring,
-    across,
     t0,
     t1,
     t2,
@@ -112,13 +112,14 @@
     face_recv,
     pair_send,
     pair_recv,
+    own_sem,
 ):
     me = lax.axis_index("owner")
     parity = me % 2
     partner = me + 1 - 2 * parity
     moving = 1 - parity
-    up1, up2 = (me + 1) % owners, (me + 2) % owners
-    dn1, dn2 = (me + owners - 1) % owners, (me + owners - 2) % owners
+    reach = [(me + by) % owners for by in (1, -1, 2, -2)]
+    exists = [me + 1 < owners, me >= 1, me + 2 < owners, me >= 2]
     stages = (x_buf, s2_buf, s3_buf, s4_buf)
     strips = (t0, t1, t2, t3)
     faces = (f0, f1, f2, f3)
@@ -143,8 +144,12 @@
     land_load = pltpu.make_async_copy(land_ref, land.at[pl.ds(0, 3)], land_sem)
     land_load.start()
     barrier = pltpu.get_barrier_semaphore()
-    for other in (up1, dn1, up2, dn2):
-        pl.semaphore_signal(barrier, inc=1, device_id=(other,), device_id_type=MESH)
+    for n in range(4):
+
+        @pl.when(exists[n])
+        def _(n=n):
+            pl.semaphore_signal(barrier, inc=1, device_id=(reach[n],), device_id_type=MESH)
+
 
     shape = (SIDE, SIDE)
     columns_up = prolong_weights(iota(shape, 1), iota(shape, 0) & (HALF - 1))
@@ -164,30 +169,35 @@
                         buf[i, c, y, x, 0:PAD] = jnp.zeros((PAD, HALF), jnp.float32)
                         buf[i, c, y, x, PAD + HALF :] = jnp.zeros((PAD, HALF), jnp.float32)
 
-    def send_faces(s, start):
+    def face_copies(s):
         f = faces[s]
-        copies = [
-            (f.at[pl.ds(3, 2)], f.at[pl.ds(1, 2)], up1),
-            (f.at[pl.ds(3, 2)], f.at[pl.ds(5, 2)], dn1),
-            (f.at[4], f.at[0], up2),
-            (f.at[3], f.at[7], dn2),
+        ends = [
+            (f.at[pl.ds(3, 2)], f.at[pl.ds(1, 2)]),
+            (f.at[pl.ds(3, 2)], f.at[pl.ds(5, 2)]),
+            (f.at[4], f.at[0]),
+            (f.at[3], f.at[7]),
         ]
         made = []
-        for n, (src, dst, to) in enumerate(copies):
+        for n, (src, dst) in enumerate(ends):
             made.append(
                 pltpu.make_async_remote_copy(
                     src_ref=src,
                     dst_ref=dst,
                     send_sem=face_send.at[s, n],
                     recv_sem=face_recv.at[s, n],
-                    device_id=(to,),
+                    device_id=(reach[n],),
                     device_id_type=MESH,
                 )
             )
-        if start:
-            for copy in made:
-                copy.start()
         return made
+
+    def send_faces(s):
+        for n, copy in enumerate(face_copies(s)):
+            pl.when(exists[n])(copy.start)
+
+    def await_faces(s):
+        for n, copy in enumerate(face_copies(s)):
+            pl.when(exists[n ^ 1])(copy.wait_recv)
 
     def put_faces(s, c, block):
         for i in range(2):
@@ -210,8 +220,8 @@
         t0[c] = block
         put_faces(0, c, block)
 
-    pl.semaphore_wait(barrier, 4)
-    sent = send_faces(0, True)
+    pl.semaphore_wait(barrier, sum(jnp.where(there, 1, 0) for there in exists))
+    send_faces(0)
     land_copy = pltpu.make_async_remote_copy(
         src_ref=land_ref.at[2 * (1 - parity)],
         dst_ref=land.at[3],
@@ -388,33 +398,32 @@
                 for j in range(2):
                     result[i, c, j, pl.ds(y, HALF, stride=2), :] = woven[:, j * HALF : (j + 1) * HALF]
 
-    result_copy = pltpu.make_async_remote_copy(
-        src_ref=result.at[moving],
-        dst_ref=result.at[2],
-        send_sem=pair_send.at[1],
-        recv_sem=pair_recv.at[1],
-        device_id=(partner,),
-        device_id_type=MESH,
-    )
-    ring_copy = pltpu.make_async_remote_copy(
-        src_ref=ring.at[moving],
-        dst_ref=ring.at[2],
-        send_sem=pair_send.at[2],
-        recv_sem=pair_recv.at[2],
-        device_id=(partner,),
-        device_id_type=MESH,
-    )
+    def to_partner(n, src, dst):
+        return pltpu.make_async_remote_copy(
+            src_ref=src.at[moving],
+            dst_ref=dst.at[2],
+            send_sem=pair_send.at[n],
+            recv_sem=pair_recv.at[n],
+            device_id=(partner,),
+            device_id_type=MESH,
+        )
+
+    result_copy = to_partner(1, result, result_out)
+    ring_copy = to_partner(2, ring, ring_out)
+    own_copies = []
+    for i in range(2):
+        own_copies.append(pltpu.make_async_copy(result.at[i], result_out.at[i], own_sem.at[i]))
+    own_copies.append(pltpu.make_async_copy(ring, ring_out.at[pl.ds(0, 2)], own_sem.at[2]))
     gaps = (
         ((moving, 0), (moving, 1), (moving, 2)),
         ((moving, 3), (moving, 4), (parity, 0)),
         ((parity, 1), (parity, 2), (parity, 3), (parity, 4)),
     )
     for s in range(4):
-        for copy in sent[4 * s : 4 * s + 4]:
-            copy.wait_recv()
+        await_faces(s)
         strip_stage(s)
         if s < 3:
-            sent = sent + send_faces(s + 1, True)
+            send_faces(s + 1)
             for i, stage in gaps[s]:
                 if stage < 4:
                     bulk_stage(i, stage)
@@ -423,56 +432,112 @@
                 if s == 1 and stage == 4:
                     result_copy.start()
     ring_copy.start()
-
-    def turn(e):
+    for copy in own_copies:
+        copy.start()
+    for s in range(4):
+        for n, copy in enumerate(face_copies(s)):
+            pl.when(exists[n])(copy.wait_send)
+    land_copy.wait_send()
+    for copy in own_copies:
+        copy.wait()
+    result_copy.wait()
+    ring_copy.wait()
+
+
+def merge_kernel(
+    counts_hbm,
+    result_hbm,
+    ring_hbm,
+    out_hbm,
+    counts_ref,
+    result,
+    ring,
+    zeros,
+    count_sem,
+    ring_sem,
+    result_sem,
+    out_sem,
+    zero_sem,
+):
+    me = lax.axis_index("owner")
+    even = me % 2 == 0
+    count_copy = pltpu.make_async_copy(counts_hbm, counts_ref, count_sem)
+    ring_copy = pltpu.make_async_copy(ring_hbm, ring, ring_sem)
+    count_copy.start()
+    ring_copy.start()
+
+    def load(e, c):
+        return pltpu.make_async_copy(result_hbm.at[e, c], result.at[e, c], result_sem.at[e, c])
+
+    for e in range(3):
         for c in range(3):
-            block = jnp.concatenate(
-                [ring[e, c, 0], jnp.zeros((HALF - 16, SIDE), jnp.float32), ring[e, c, 1]], axis=0
-            )
-            across[e, c, 0:HALF] = block[:, :HALF].T
-            across[e, c, HALF:SIDE] = block[:, HALF:].T
-
-    turn(0)
-    turn(1)
-    result_copy.wait_recv()
-    ring_copy.wait_recv()
-    turn(2)
-
+            load(e, c).start()
+    zeros[...] = jnp.zeros_like(zeros)
+    count_copy.wait()
+    count = counts_ref[me]
+    empties = []
+    for s in (1, 2):
+        empties.append(pltpu.make_async_copy(zeros, out_hbm.at[s], zero_sem.at[s - 1]))
+        pl.when(s >= count)(empties[-1].start)
+
+    slots = []
+    for e in range(3):
+        slot = jnp.where(even, e, (e + 1) % 3 + count - 3)
+        slots.append((slot, (slot >= 0) & (slot < count)))
     low_lanes = iota((8, HALF), 1) < 4
     high_lanes = iota((8, HALF), 1) >= HALF - 4
-    sub_rows = iota((8, SIDE), 0)
-    sources = []
-    for s in range(3):
-        from_even = s
-        from_odd = (5 - count + s) % 3
-        sources.append((jnp.where(parity == 0, from_even, from_odd), s < count))
-
-    def place(step, carry):
-        r = pl.multiple_of(step * 8, 8)
-        for s in range(3):
-            e, held = sources[s]
+    sub_rows = iota((8, HALF), 0)
+    ring_copy.wait()
+
+    def stores(e, c):
+        made = []
+        for j in range(2):
+            made.append(
+                pltpu.make_async_copy(
+                    result.at[e, c, j],
+                    out_hbm.at[jnp.maximum(slots[e][0], 0), c, :, pl.ds(j * HALF, HALF)],
+                    out_sem.at[e, c, j],
+                )
+            )
+        return made
+
+    for e in range(3):
+        for c in range(3):
+            gap = jnp.zeros((HALF - 16, SIDE), jnp.float32)
+            block = jnp.concatenate([ring[e, c, 0], gap, ring[e, c, 1]], axis=0)
+            sides = (block[:, :HALF].T, block[:, HALF:].T)
+            load(e, c).wait()
+            for j in range(2):
+                lanes = high_lanes if j else low_lanes
+                for t in range(SIDE // 8):
+                    rows = slice(8 * t, 8 * t + 8)
+                    within = slice(8 * t % HALF, 8 * t % HALF + 8)
+                    value = jnp.where(lanes, sides[t // 16][within], result[e, c, j, rows, :])
+                    if t == 0:
+                        value = jnp.where(
+                            sub_rows < 4, ring[e, c, 2, :, j * HALF : (j + 1) * HALF], value
+                        )
+                    if t == SIDE // 8 - 1:
+                        value = jnp.where(
+                            sub_rows >= 4, ring[e, c, 3, :, j * HALF : (j + 1) * HALF], value
+                        )
+                    result[e, c, j, rows, :] = value
+
+            @pl.when(slots[e][1])
+            def _(e=e, c=c):
+                for copy in stores(e, c):
+                    copy.start()
+
+    for e in range(3):
+
+        @pl.when(slots[e][1])
+        def _(e=e):
             for c in range(3):
-                side = across[e, c, pl.ds(r, 8), :]
-                left = jnp.where(low_lanes, side, result[e, c, 0, pl.ds(r, 8), :])
-                right = jnp.where(high_lanes, side, result[e, c, 1, pl.ds(r, 8), :])
-                out_ref[s, c, pl.ds(r, 8), 0:HALF] = jnp.where(held, left, 0.0)
-                out_ref[s, c, pl.ds(r, 8), HALF:SIDE] = jnp.where(held, right, 0.0)
-        return carry
-
-    lax.fori_loop(0, SIDE // 8, place, 0)
-    for s in range(3):
-        e, held = sources[s]
-        for c in range(3):
-            for n, rows in ((0, slice(0, 8)), (1, slice(SIDE - 8, SIDE))):
-                inside = sub_rows < 4 if n == 0 else sub_rows >= 4
-                merged = jnp.where(inside, ring[e, c, 2 + n], out_ref[s, c, rows, :])
-                out_ref[s, c, rows, :] = jnp.where(held, merged, 0.0)
-
-    for copy in sent:
-        copy.wait_send()
-    land_copy.wait_send()
-    result_copy.wait_send()
-    ring_copy.wait_send()
+                for copy in stores(e, c):
+                    copy.wait()
+
+    for s in (1, 2):
+        pl.when(s >= count)(empties[s - 1].wait)
 
 
 def body(coarse, parents, new_counts, neighbours, land_cover, class_diffusivity, class_growth):
@@ -482,11 +547,13 @@
     stage_buf = pltpu.VMEM((2, 3, 2, 2, HALF + 2 * PAD, HALF), f32)
     strip_buf = pltpu.VMEM((3, 8, 8, SIDE), f32)
     face_buf = pltpu.VMEM((8, 16, SIDE), f32)
-    return pl.pallas_call(
+    results = jax.ShapeDtypeStruct((3, 3, 2, SIDE, HALF), f32)
+    rings = jax.ShapeDtypeStruct((3, 3, 4, 8, SIDE), f32)
+    whole, outer = pl.pallas_call(
         functools.partial(kernel, owners),
-        out_shape=jax.ShapeDtypeStruct((3, 3, SIDE, SIDE), f32),
+        out_shape=(results, rings),
         in_specs=[hbm] * 7,
-        out_specs=pl.BlockSpec(memory_space=pltpu.VMEM),
+        out_specs=(hbm, hbm),
         scratch_shapes=[
             pltpu.SMEM((2,), jnp.int32),
             pltpu.SMEM((owners,), jnp.int32),
@@ -501,9 +568,8 @@
             stage_buf,
             pltpu.VMEM((2, 2, 2, HALF, HALF), f32),
             pltpu.VMEM((2, 2, 2, HALF, HALF), f32),
-            pltpu.VMEM((3, 3, 2, SIDE, HALF), f32),
-            pltpu.VMEM((3, 3, 4, 8, SIDE), f32),
-            pltpu.VMEM((3, 3, SIDE, HALF), f32),
+            pltpu.VMEM((2, 3, 2, SIDE, HALF), f32),
+            pltpu.VMEM((2, 3, 4, 8, SIDE), f32),
             strip_buf,
             strip_buf,
             strip_buf,
@@ -521,12 +587,32 @@
             pltpu.SemaphoreType.DMA((4, 4)),
             pltpu.SemaphoreType.DMA((3,)),
             pltpu.SemaphoreType.DMA((3,)),
+            pltpu.SemaphoreType.DMA((3,)),
         ],
         compiler_params=pltpu.CompilerParams(
             collective_id=0, has_side_effects=True, vmem_limit_bytes=62 * 1024 * 1024
         ),
         name="regrid_step",
     )(parents, new_counts, neighbours.T, class_diffusivity, class_growth, coarse, land_cover)
+    return pl.pallas_call(
+        merge_kernel,
+        out_shape=jax.ShapeDtypeStruct((3, 3, SIDE, SIDE), f32),
+        in_specs=[hbm] * 3,
+        out_specs=hbm,
+        scratch_shapes=[
+            pltpu.SMEM((owners,), jnp.int32),
+            pltpu.VMEM(results.shape, f32),
+            pltpu.VMEM(rings.shape, f32),
+            pltpu.VMEM((3, SIDE, SIDE), f32),
+            pltpu.SemaphoreType.DMA,
+            pltpu.SemaphoreType.DMA,
+            pltpu.SemaphoreType.DMA((3, 3)),
+            pltpu.SemaphoreType.DMA((3, 3, 2)),
+            pltpu.SemaphoreType.DMA((2,)),
+        ],
+        compiler_params=pltpu.CompilerParams(vmem_limit_bytes=62 * 1024 * 1024),
+        name="merge_slots",
+    )(new_counts, whole, outer)
 
 
 def solution(mesh):

time: 41 us -> 33.7 us (0.82)
  the two profiles are of different devices: /device:TPU:1 before, /device:TPU:25 now
where the time goes in v2:
time: 33.7 us; the launch traced here: 33.6 us
  Pallas kernels  33.6 us (100%)
    pallas_call x1, Pallas kernels, body(): pl.pallas_call(functools.partial(kernel, owners), out_shape=(results, rin...  30.1 us
    pallas_call x1, Pallas kernels, body(): pl.pallas_call(merge_kernel, out_shape=jax.ShapeDtypeStruct((3, 3, SIDE,...  3.5 us

profile of v2, /device:TPU:25, one launch (start us, length us, event | category | flops | bytes accessed | tf_op | source)
XLA Modules:
  0.0 33.6 jit_solution(6817642613809697947)
XLA Ops:
  0.0 30.1 %regrid_step.1 = (f32[3,3,2,256,128]{4,3,2,1,0:T(8,128)}, f32[3,3,4,8,256]{4,3,2,1,0:T(8,128)}) custom-call(s32[2]{0:T(128)} %parents_hbm.1, s32[128]{0:T(128)} %counts_hbm.3, s32[4,256]{1,0:T(4,128)} %bitcast.1, f32[11]{0:T(128)} %diff_hbm.1, f32[11]{0:T(128)} %grow_hbm.1, f32[1,3,256,256]{3,2,1,0:T(8,128)} %coarse_ref.1, s32[3,256,256]{2,1,0:T(8,128)} %land_ref.1), custom_call_target="tpu_custom_call" | custom-call | tf_op jit(solution)/shard_map/regrid_step/pallas_call | solution.py:552
  30.1 3.5 %merge_slots.1 = f32[3,3,256,256]{3,2,1,0:T(8,128)} custom-call(s32[128]{0:T(128)} %counts_hbm.3, f32[3,3,2,256,128]{4,3,2,1,0:T(8,128)} %get-tuple-element.7.result_hbm, f32[3,3,4,8,256]{4,3,2,1,0:T(8,128)} %get-tuple-element.8.ring_hbm), custom_call_target="tpu_custom_call" | custom-call | tf_op jit(solution)/shard_map/merge_slots/pallas_call | solution.py:597

commit v3 on v2

--- a/solution.py
+++ b/solution.py
@@ -11,6 +11,7 @@
 HALF = 128
 CLASSES = 11
 PAD = 8
+REACH = 6
 WEIGHTS = (0.5, 0.5, 1.0, 1.0 / 6.0)
 MESH = pl.DeviceIdType.MESH
 
@@ -45,14 +46,31 @@
     return lax.dot_general(a, b, (((1,), (1,)), ((), ())), preferred_element_type=jnp.float32)
 
 
-def look_up(classes, diff_ref, grow_ref):
-    diffus = jnp.full(classes.shape, diff_ref[0], jnp.float32)
-    growth = jnp.full(classes.shape, grow_ref[0], jnp.float32)
-    for number in range(1, CLASSES):
-        hit = classes == jnp.asarray(number, classes.dtype)
-        diffus = jnp.where(hit, diff_ref[number], diffus)
-        growth = jnp.where(hit, grow_ref[number], growth)
-    return diffus, growth
+def table_of(ref):
+    lane = iota((8, HALF), 1)
+    table = jnp.zeros((8, HALF), jnp.float32)
+    for number in range(CLASSES):
+        table = jnp.where(lane == number, ref[number], table)
+    return table
+
+
+def pick_lanes(table, index):
+    return jnp.take_along_axis(table, index, axis=1)
+
+
+def look_up(classes, tables):
+    index = classes.astype(jnp.int32)
+    rows, columns = classes.shape
+    found = []
+    for table in tables:
+        bands = []
+        for r in range(0, rows, 8):
+            blocks = [
+                pick_lanes(table, index[r : r + 8, k : k + HALF]) for k in range(0, columns, HALF)
+            ]
+            bands.append(jnp.concatenate(blocks, axis=1))
+        found.append(jnp.concatenate(bands, axis=0))
+    return found
 
 
 def scaled_rates(weight, x0, x1, x2, lap0, lap1, lap2, diffus, growth):
@@ -101,15 +119,26 @@
     t3,
     strip_diffus,
     strip_growth,
-    f0,
-    f1,
-    f2,
-    f3,
+    face_data,
+    corner_data,
+    h0,
+    h1,
+    h2,
+    h3,
+    outer_diffus,
+    outer_growth,
+    l0,
+    l1,
+    far_diffus,
+    far_growth,
+    k0,
     load_sem,
     small_sem,
     land_sem,
     face_send,
     face_recv,
+    corner_send,
+    corner_recv,
     pair_send,
     pair_recv,
     own_sem,
@@ -118,11 +147,12 @@
     parity = me % 2
     partner = me + 1 - 2 * parity
     moving = 1 - parity
-    reach = [(me + by) % owners for by in (1, -1, 2, -2)]
-    exists = [me + 1 < owners, me >= 1, me + 2 < owners, me >= 2]
+    steps = [by for far in range(1, REACH + 1) for by in (far, -far)]
+    reach = [(me + by) % owners for by in steps]
+    exists = [(me + by < owners) & (me + by >= 0) for by in steps]
     stages = (x_buf, s2_buf, s3_buf, s4_buf)
     strips = (t0, t1, t2, t3)
-    faces = (f0, f1, f2, f3)
+    outer = (h0, h1, h2, h3)
 
     loads = []
     for q in range(4):
@@ -144,7 +174,7 @@
     land_load = pltpu.make_async_copy(land_ref, land.at[pl.ds(0, 3)], land_sem)
     land_load.start()
     barrier = pltpu.get_barrier_semaphore()
-    for n in range(4):
+    for n in range(len(steps)):
 
         @pl.when(exists[n])
         def _(n=n):
@@ -158,8 +188,12 @@
     weave = jnp.where(phased(iota(shape, 0)) == iota(shape, 1), 1.0, 0.0).astype(jnp.bfloat16)
     unweave = jnp.where(phased(iota(shape, 1)) == iota(shape, 0), 1.0, 0.0).astype(jnp.bfloat16)
     edge = iota((16, SIDE), 0)
-    edge = jnp.where(edge < 8, edge, edge + (SIDE - 16))
+    edge = jnp.where(edge < 8, edge, SIDE + 7 - edge)
     edge_up = prolong_weights(edge, iota((16, SIDE), 1) & (HALF - 1))
+    rim = iota((16, SIDE), 0)
+    rim = jnp.where(rim < 8, rim, HALF + 7 - rim)
+    rim_pick = jnp.where((iota((16, SIDE), 1) & (HALF - 1)) == rim, 1.0, 0.0).astype(jnp.bfloat16)
+    edge_and_rim = jnp.concatenate([edge_up, rim_pick], axis=0)
     edge_pick = jnp.where(iota((16, SIDE), 1) == edge, 1.0, 0.0).astype(jnp.bfloat16)
     for buf in stages:
         for i in range(2):
@@ -169,13 +203,12 @@
                         buf[i, c, y, x, 0:PAD] = jnp.zeros((PAD, HALF), jnp.float32)
                         buf[i, c, y, x, PAD + HALF :] = jnp.zeros((PAD, HALF), jnp.float32)
 
-    def face_copies(s):
-        f = faces[s]
+    def face_copies():
         ends = [
-            (f.at[pl.ds(3, 2)], f.at[pl.ds(1, 2)]),
-            (f.at[pl.ds(3, 2)], f.at[pl.ds(5, 2)]),
-            (f.at[4], f.at[0]),
-            (f.at[3], f.at[7]),
+            (face_data.at[pl.ds(3, 2)], face_data.at[pl.ds(1, 2)]),
+            (face_data.at[pl.ds(3, 2)], face_data.at[pl.ds(5, 2)]),
+            (face_data.at[4], face_data.at[0]),
+            (face_data.at[3], face_data.at[7]),
         ]
         made = []
         for n, (src, dst) in enumerate(ends):
@@ -183,27 +216,28 @@
                 pltpu.make_async_remote_copy(
                     src_ref=src,
                     dst_ref=dst,
-                    send_sem=face_send.at[s, n],
-                    recv_sem=face_recv.at[s, n],
+                    send_sem=face_send.at[n],
+                    recv_sem=face_recv.at[n],
                     device_id=(reach[n],),
                     device_id_type=MESH,
                 )
             )
         return made
 
-    def send_faces(s):
-        for n, copy in enumerate(face_copies(s)):
-            pl.when(exists[n])(copy.start)
-
-    def await_faces(s):
-        for n, copy in enumerate(face_copies(s)):
-            pl.when(exists[n ^ 1])(copy.wait_recv)
-
-    def put_faces(s, c, block):
-        for i in range(2):
-            for f in range(4):
-                row = 7 * (f % 2)
-                faces[s][3 + i, 4 * f + c : 4 * f + c + 1, :] = block[4 * i + f, row : row + 1, :]
+    def corner_copies():
+        made = []
+        for n, by in enumerate(steps):
+            made.append(
+                pltpu.make_async_remote_copy(
+                    src_ref=corner_data.at[REACH, pl.ds(0, 4)],
+                    dst_ref=corner_data.at[REACH - by, pl.ds(0, 4)],
+                    send_sem=corner_send.at[n],
+                    recv_sem=corner_recv.at[n],
+                    device_id=(reach[n],),
+                    device_id_type=MESH,
+                )
+            )
+        return made
 
     for load in loads + small:
         load.wait()
@@ -212,16 +246,17 @@
     for i in range(2):
         for c in range(3):
             block = quads[parent[i], c]
-            edges.append(dot_t(edge_up, split(block, 1)))
-            edges.append(dot(edge_up, split(block, 0)))
+            across = dot_t(edge_and_rim, split(block, 1))
+            along = dot(edge_and_rim, split(block, 0))
+            edges += [across[0:16], along[0:16]]
+            for f in range(4):
+                rows = (across, along)[f // 2][16 + 8 * (f % 2) : 19 + 8 * (f % 2)]
+                face_data[3 + i, f, 3 * c : 3 * c + 3, :] = rows
     edges = dot(split(jnp.concatenate(edges, axis=0), 1), columns_up).reshape(2, 3, 4, 8, SIDE)
     for c in range(3):
-        block = jnp.concatenate([edges[0, c], edges[1, c]], axis=0)
-        t0[c] = block
-        put_faces(0, c, block)
+        t0[c] = jnp.concatenate([edges[0, c], edges[1, c]], axis=0)
 
     pl.semaphore_wait(barrier, sum(jnp.where(there, 1, 0) for there in exists))
-    send_faces(0)
     land_copy = pltpu.make_async_remote_copy(
         src_ref=land_ref.at[2 * (1 - parity)],
         dst_ref=land.at[3],
@@ -250,35 +285,61 @@
         even_slot = jnp.where(i >= count, 3, i)
         odd_slot = jnp.where(i - 2 + count < 0, 3, i - 2 + count)
         slots.append(jnp.where(parity == 0, even_slot, odd_slot))
+    tables = (table_of(diff_ref), table_of(grow_ref))
+    classes_of = []
     for i in range(2):
         classes = land[slots[i]].astype(jnp.float32).astype(jnp.bfloat16)
-        picked = dot_t(edge_pick, classes)
-        across_d, across_g = look_up(picked, diff_ref, grow_ref)
-        ends = jnp.concatenate(
-            [land[slots[i], 0:8, :], land[slots[i], SIDE - 8 : SIDE, :]], axis=0
-        )
-        along_d, along_g = look_up(ends, diff_ref, grow_ref)
-        for n in range(2):
-            rows = slice(8 * n, 8 * n + 8)
-            strip_diffus[4 * i + n] = across_d[rows]
-            strip_growth[4 * i + n] = across_g[rows]
-            strip_diffus[4 * i + 2 + n] = along_d[rows]
-            strip_growth[4 * i + 2 + n] = along_g[rows]
-
-        classes = dot(classes, unweave).astype(jnp.bfloat16)
+        classes_of.append(classes)
+        rims = jnp.concatenate([dot_t(edge_pick, classes), dot(edge_pick, classes)], axis=0)
+        d, g = look_up(rims, tables)
+        for f in range(4):
+            rows = slice(8 * f, 8 * f + 8)
+            strip_diffus[4 * i + f] = d[rows]
+            strip_growth[4 * i + f] = g[rows]
+            for a in range(3):
+                for j in range(2):
+                    at = 9 + 2 * a + j
+                    row = 8 * f + a
+                    face_data[3 + i, f, at : at + 1, :] = rims[
+                        row : row + 1, j * HALF : (j + 1) * HALF
+                    ]
+
+    lane8, sub8 = iota((8, HALF), 1), iota((8, HALF), 0)
+    for i in range(2):
+        for x in range(2):
+            row = jnp.zeros((8, HALF), jnp.float32)
+            for q in range(5):
+                pf = 4 * i + x
+                strip_of = t0[q, pf] if q < 3 else (strip_diffus, strip_growth)[q - 3][pf]
+                for y in range(2):
+                    cell = lane8 - (64 * y + 9 * q + 3 * sub8)
+                    inside = (cell >= 0) & (cell < 3) & (sub8 < 3)
+                    cell = jnp.clip(cell, 0, 2)
+                    cell = HALF - 1 - cell if y else cell
+                    part = pick_lanes(strip_of[:, y * HALF : (y + 1) * HALF], cell)
+                    row = row + jnp.where(inside, part, 0.0)
+            at = 2 * i + x
+            corner_data[REACH, at : at + 1, :] = jnp.sum(row, axis=0, keepdims=True)
+
+    for n, copy in enumerate(face_copies()):
+        pl.when(exists[n])(copy.start)
+    for n, copy in enumerate(corner_copies()):
+        pl.when(exists[n])(copy.start)
+
+    for i in range(2):
+        classes = dot(classes_of[i], unweave).astype(jnp.bfloat16)
         for n in range(8):
             rows = slice(32 * n, 32 * n + 32)
-            d, g = look_up(dot(weave[rows], classes), diff_ref, grow_ref)
+            d, g = look_up(dot(weave[rows], classes), tables)
             y, m = n // 4, 32 * (n % 4)
             for x in range(2):
                 diffus_buf[i, y, x, m : m + 32] = d[:, x * HALF : (x + 1) * HALF]
                 growth_buf[i, y, x, m : m + 32] = g[:, x * HALF : (x + 1) * HALF]
 
-    peers = []
-    for i in range(2):
-        for f in range(4):
-            value = nb_ref[f, 2 * me + i]
-            peers.append((value >= 0, jnp.clip(value - (2 * me - 3), 0, 7)))
+    def cross(patch, face):
+        value = nb_ref[face, patch]
+        has = value >= 0
+        return jnp.where(has, value, patch), jnp.where(has, face ^ 1, face)
 
     strip = (8, 8, SIDE)
     sub = iota(strip, 1)
@@ -286,25 +347,94 @@
     sub_half = iota((8, 8, HALF), 1)
     lane_half = iota((8, 8, HALF), 2)
 
-    def strip_laplacian(s, c):
-        now = strips[s][c]
-        f_ref = faces[s]
-        ghosts = []
+    def gather_outer():
+        first = [
+            jnp.where(sub8 == 0, 1.0, jnp.where(sub8 == 1, 0.75, jnp.where(sub8 == 2, 0.25, 0.0))),
+            jnp.where(sub8 == 0, 0.0, jnp.where(sub8 == 1, 0.25, 0.75)),
+            jnp.where(sub8 >= 3, 0.25, 0.0),
+        ]
+        index = {}
+        for kind in range(2):
+            for e in range(2):
+                b = jnp.minimum(lane8 if e else HALF - 1 - lane8, 2)
+                a = jnp.minimum(sub8, 2)
+                index[kind, e] = 3 * a + b if kind == 0 else 3 * b + a
+        walls, classes = [], []
         for i in range(2):
             for f in range(4):
-                has, where = peers[4 * i + f]
-                theirs = 4 * (f ^ 1) + c
-                ours = 4 * f + c
-                row = jnp.where(
-                    has, f_ref[where, theirs : theirs + 1, :], f_ref[3 + i, ours : ours + 1, :]
-                )
-                ghosts.append(jnp.broadcast_to(row, (8, SIDE)))
-        ghost = jnp.stack(ghosts, axis=0)
+                patch, face = cross(2 * me + i, f)
+                where = jnp.clip(patch - (2 * me - 3), 0, 7)
+                for c in range(3):
+                    parts = []
+                    for a in range(3):
+                        at = 3 * c + a
+                        row = face_data[where, face, at : at + 1, :]
+                        parts.append(first[a] * jnp.broadcast_to(row, (8, HALF)))
+                    walls.append(parts[0] + parts[1] + parts[2])
+                for j in range(2):
+                    rows = []
+                    for a in range(3):
+                        at = 9 + 2 * a + j
+                        rows.append(
+                            jnp.broadcast_to(face_data[where, face, at : at + 1, :], (8, HALF))
+                        )
+                    classes.append(jnp.where(sub8 == 0, rows[0], jnp.where(sub8 == 1, rows[1], rows[2])))
+        walls = dot(split(jnp.concatenate(walls, axis=0), 1), columns_up).reshape(8, 3, 8, SIDE)
+        d, g = look_up(jnp.concatenate(classes, axis=0), tables)
+        d, g = d.reshape(8, 2, 8, HALF), g.reshape(8, 2, 8, HALF)
+        for c in range(3):
+            h0[c, :, :, HALF : HALF + SIDE] = walls[:, c]
+        for j in range(2):
+            at = slice(HALF + j * HALF, 2 * HALF + j * HALF)
+            outer_diffus[:, :, at] = d[:, j]
+            outer_growth[:, :, at] = g[:, j]
+
+        for i in range(2):
+            for f in range(4):
+                pf = 4 * i + f
+                kind = f // 2
+                for e in range(2):
+                    patch, wall = cross(2 * me + i, f)
+                    side = 2 * (1 - kind) + e
+                    for step in range(3):
+                        if step % 2 == 0:
+                            patch, side = cross(patch, side)
+                        else:
+                            patch, wall = cross(patch, wall)
+                        x = wall if kind == 0 else side
+                        y = (side if kind == 0 else wall) - 2
+                        window = jnp.clip((patch >> 1) - me + REACH, 0, 2 * REACH)
+                        row = corner_data[window, pl.ds(2 * (patch & 1) + x, 1), :]
+                        row = jnp.broadcast_to(row, (8, HALF))
+                        row = jnp.where(y == 1, pltpu.roll(row, 64, 1), row)
+                        for q in range(5 if step < 2 else 3):
+                            if step < 2:
+                                tile = pick_lanes(row, index[kind, e] + 9 * q)
+                            else:
+                                tile = pick_lanes(row, jnp.full((8, HALF), 9 * q, jnp.int32))
+                            near = slice(3 * HALF * e, 3 * HALF * e + HALF)
+                            far = slice(HALF * e, HALF * e + HALF)
+                            if step == 0 and q < 3:
+                                h0[q, pf, :, near] = tile
+                            elif step == 0:
+                                (outer_diffus, outer_growth)[q - 3][pf, :, near] = tile
+                            elif step == 1 and q < 3:
+                                l0[q, pf, :, far] = tile
+                            elif step == 1:
+                                (far_diffus, far_growth)[q - 3][pf, :, far] = tile
+                            else:
+                                k0[q, pf, :, far] = tile
+
+    def rates_of(s, now, laps, diffus, growth):
+        return scaled_rates(WEIGHTS[s], *now, *laps, diffus, growth)
+
+    def strip_laplacian(now, beyond):
+        ghost = jnp.broadcast_to(beyond[:, 0:1, :], strip)
         low = jnp.sum(
             jnp.where(lane_half == sub_half, ghost[:, :, :HALF], 0.0), axis=2, keepdims=True
         )
         high = jnp.sum(
-            jnp.where(lane_half == sub_half + (HALF - 8), ghost[:, :, HALF:], 0.0),
+            jnp.where(lane_half == HALF - 1 - sub_half, ghost[:, :, HALF:], 0.0),
             axis=2,
             keepdims=True,
         )
@@ -313,34 +443,77 @@
             columns = []
             for i in range(2):
                 for f in range(4):
-                    source = (low, high)[f % 2]
                     face = 4 * i + (2 if f < 2 else 0) + e
-                    columns.append(source[face])
+                    columns.append((low, high)[f % 2][face])
             ends.append(jnp.stack(columns, axis=0))
         above = jnp.where(sub == 0, ghost, pltpu.roll(now, 1, 1))
-        below = jnp.where(sub == 7, ghost, pltpu.roll(now, 7, 1))
+        below = pltpu.roll(now, 7, 1)
         left = jnp.where(lane == 0, ends[0], pltpu.roll(now, 1, 2))
         right = jnp.where(lane == SIDE - 1, ends[1], pltpu.roll(now, SIDE - 1, 2))
-        return now, (left + right) + (below + above) - 4.0 * now
+        return (left + right) + (below + above) - 4.0 * now
+
+    wide = (8, 8, 2 * SIDE)
+
+    def wide_laplacian(now, facing):
+        above = jnp.where(iota(wide, 1) == 0, facing, pltpu.roll(now, 1, 1))
+        below = pltpu.roll(now, 7, 1)
+        sides = pltpu.roll(now, 1, 2) + pltpu.roll(now, 2 * SIDE - 1, 2)
+        return sides + (below + above) - 4.0 * now
+
+    def two_ends(block):
+        return jnp.concatenate([block[:, :, :HALF], block[:, :, HALF + SIDE :]], axis=2)
+
+    def between(ends, middle):
+        return jnp.concatenate([ends[:, :, :HALF], middle, ends[:, :, HALF:]], axis=2)
+
+    middle = slice(HALF, HALF + SIDE)
 
     def strip_stage(s):
-        values = [strip_laplacian(s, c) for c in range(3)]
-        rates = scaled_rates(
-            WEIGHTS[s],
-            *[v[0] for v in values],
-            *[v[1] for v in values],
-            strip_diffus[...],
-            strip_growth[...],
-        )
-        for c in range(3):
-            if s < 3:
-                block = t0[c] + rates[c]
-                strips[s + 1][c] = block
-                put_faces(s + 1, c, block)
-            else:
+        inner = [strips[s][c] for c in range(3)]
+        beyond = [outer[s][c, :, :, middle] for c in range(3)]
+        laps = [strip_laplacian(inner[c], beyond[c]) for c in range(3)]
+        rates = rates_of(s, inner, laps, strip_diffus[...], strip_growth[...])
+        if s == 3:
+            for c in range(3):
                 block = combine(t0[c], t1[c], t2[c], t3[c], rates[c])
                 for i in range(2):
                     ring[i, c] = block[4 * i : 4 * i + 4]
+                    for f in (1, 3):
+                        for r in range(4):
+                            ring[i, c, f, 7 - r : 8 - r, :] = block[4 * i + f, r : r + 1, :]
+            return
+        for c in range(3):
+            strips[s + 1][c] = t0[c] + rates[c]
+        if s == 2:
+            now = beyond
+            laps = []
+            for c in range(3):
+                whole = outer[s][c]
+                above = jnp.where(sub == 0, inner[c], pltpu.roll(now[c], 1, 1))
+                sides = pltpu.roll(whole, 1, 2) + pltpu.roll(whole, 2 * SIDE - 1, 2)
+                laps.append(
+                    sides[:, :, middle] + (pltpu.roll(now[c], 7, 1) + above) - 4.0 * now[c]
+                )
+            rates = rates_of(
+                s, now, laps, outer_diffus[:, :, middle], outer_growth[:, :, middle]
+            )
+            for c in range(3):
+                outer[3][c, :, :, middle] = h0[c, :, :, middle] + rates[c]
+            return
+        far = [(l0, l1)[s][c] for c in range(3)]
+        now = [outer[s][c] for c in range(3)]
+        laps = [wide_laplacian(now[c], between(far[c], inner[c])) for c in range(3)]
+        rates = rates_of(s, now, laps, outer_diffus[...], outer_growth[...])
+        for c in range(3):
+            outer[s + 1][c] = h0[c] + rates[c]
+        if s == 0:
+            laps = []
+            for c in range(3):
+                lap = wide_laplacian(between(far[c], k0[c]), now[c])
+                laps.append(two_ends(lap))
+            rates = rates_of(s, far, laps, far_diffus[...], far_growth[...])
+            for c in range(3):
+                l1[c] = far[c] + rates[c]
 
     def bulk_stage(i, s):
         src = stages[s]
@@ -414,29 +587,26 @@
     for i in range(2):
         own_copies.append(pltpu.make_async_copy(result.at[i], result_out.at[i], own_sem.at[i]))
     own_copies.append(pltpu.make_async_copy(ring, ring_out.at[pl.ds(0, 2)], own_sem.at[2]))
-    gaps = (
-        ((moving, 0), (moving, 1), (moving, 2)),
-        ((moving, 3), (moving, 4), (parity, 0)),
-        ((parity, 1), (parity, 2), (parity, 3), (parity, 4)),
-    )
+    for i in (moving, parity):
+        for s in range(4):
+            bulk_stage(i, s)
+        bulk_weave(i)
+        if i is moving:
+            result_copy.start()
+    for n, copy in enumerate(face_copies()):
+        pl.when(exists[n ^ 1])(copy.wait_recv)
+    for n, copy in enumerate(corner_copies()):
+        pl.when(exists[n ^ 1])(copy.wait_recv)
+    gather_outer()
     for s in range(4):
-        await_faces(s)
         strip_stage(s)
-        if s < 3:
-            send_faces(s + 1)
-            for i, stage in gaps[s]:
-                if stage < 4:
-                    bulk_stage(i, stage)
-                else:
-                    bulk_weave(i)
-                if s == 1 and stage == 4:
-                    result_copy.start()
     ring_copy.start()
     for copy in own_copies:
         copy.start()
-    for s in range(4):
-        for n, copy in enumerate(face_copies(s)):
-            pl.when(exists[n])(copy.wait_send)
+    for n, copy in enumerate(face_copies()):
+        pl.when(exists[n])(copy.wait_send)
+    for n, copy in enumerate(corner_copies()):
+        pl.when(exists[n])(copy.wait_send)
     land_copy.wait_send()
     for copy in own_copies:
         copy.wait()
@@ -546,7 +716,7 @@
     hbm = pl.BlockSpec(memory_space=pltpu.HBM)
     stage_buf = pltpu.VMEM((2, 3, 2, 2, HALF + 2 * PAD, HALF), f32)
     strip_buf = pltpu.VMEM((3, 8, 8, SIDE), f32)
-    face_buf = pltpu.VMEM((8, 16, SIDE), f32)
+    outer_buf = pltpu.VMEM((3, 8, 8, 2 * SIDE), f32)
     results = jax.ShapeDtypeStruct((3, 3, 2, SIDE, HALF), f32)
     rings = jax.ShapeDtypeStruct((3, 3, 4, 8, SIDE), f32)
     whole, outer = pl.pallas_call(
@@ -576,15 +746,26 @@
             strip_buf,
             pltpu.VMEM((8, 8, SIDE), f32),
             pltpu.VMEM((8, 8, SIDE), f32),
-            face_buf,
-            face_buf,
-            face_buf,
-            face_buf,
+            pltpu.VMEM((8, 4, 16, HALF), f32),
+            pltpu.VMEM((2 * REACH + 1, 8, HALF), f32),
+            outer_buf,
+            outer_buf,
+            outer_buf,
+            outer_buf,
+            pltpu.VMEM((8, 8, 2 * SIDE), f32),
+            pltpu.VMEM((8, 8, 2 * SIDE), f32),
+            strip_buf,
+            strip_buf,
+            pltpu.VMEM((8, 8, SIDE), f32),
+            pltpu.VMEM((8, 8, SIDE), f32),
+            strip_buf,
             pltpu.SemaphoreType.DMA((4,)),
             pltpu.SemaphoreType.DMA((5,)),
             pltpu.SemaphoreType.DMA,
-            pltpu.SemaphoreType.DMA((4, 4)),
-            pltpu.SemaphoreType.DMA((4, 4)),
+            pltpu.SemaphoreType.DMA((4,)),
+            pltpu.SemaphoreType.DMA((4,)),
+            pltpu.SemaphoreType.DMA((2 * REACH,)),
+            pltpu.SemaphoreType.DMA((2 * REACH,)),
             pltpu.SemaphoreType.DMA((3,)),
             pltpu.SemaphoreType.DMA((3,)),
             pltpu.SemaphoreType.DMA((3,)),

time: 33.7 us -> 25.4 us (0.75)
  Pallas kernels: 33.6 us -> 25.2 us
    pallas_call x1, Pallas kernels: 30.1 us -> 22 us  [body(): pl.pallas_call(functools.partial(kernel, owners), out_shape=(results, rin...]
where the time goes in v3:
time: 25.4 us; the launch traced here: 25.2 us
  Pallas kernels  25.2 us (99%)
    pallas_call x1, Pallas kernels, body(): pl.pallas_call(functools.partial(kernel, owners), out_shape=(results, rin...  22 us
    pallas_call x1, Pallas kernels, body(): pl.pallas_call(merge_kernel, out_shape=jax.ShapeDtypeStruct((3, 3, SIDE,...  3.21 us

profile of v3, /device:TPU:25, one launch (start us, length us, event | category | flops | bytes accessed | tf_op | source)
XLA Modules:
  0.0 25.2 jit_solution(1088477333457459357)
XLA Ops:
  0.0 22.0 %regrid_step.1 = (f32[3,3,2,256,128]{4,3,2,1,0:T(8,128)}, f32[3,3,4,8,256]{4,3,2,1,0:T(8,128)}) custom-call(s32[2]{0:T(128)} %parents_hbm.1, s32[128]{0:T(128)} %counts_hbm.3, s32[4,256]{1,0:T(4,128)} %bitcast.1, f32[11]{0:T(128)} %diff_hbm.1, f32[11]{0:T(128)} %grow_hbm.1, f32[1,3,256,256]{3,2,1,0:T(8,128)} %coarse_ref.1, s32[3,256,256]{2,1,0:T(8,128)} %land_ref.1), custom_call_target="tpu_custom_call" | custom-call | tf_op jit(solution)/shard_map/regrid_step/pallas_call | solution.py:722
  22.0 3.2 %merge_slots.1 = f32[3,3,256,256]{3,2,1,0:T(8,128)} custom-call(s32[128]{0:T(128)} %counts_hbm.3, f32[3,3,2,256,128]{4,3,2,1,0:T(8,128)} %get-tuple-element.7.result_hbm, f32[3,3,4,8,256]{4,3,2,1,0:T(8,128)} %get-tuple-element.8.ring_hbm), custom_call_target="tpu_custom_call" | custom-call | tf_op jit(solution)/shard_map/merge_slots/pallas_call | solution.py:778

commit v4 on v3

--- a/solution.py
+++ b/solution.py
@@ -12,6 +12,7 @@
 CLASSES = 11
 PAD = 8
 REACH = 6
+VMEM_LIMIT = 62 * 1024 * 1024
 WEIGHTS = (0.5, 0.5, 1.0, 1.0 / 6.0)
 MESH = pl.DeviceIdType.MESH
 
@@ -239,6 +240,17 @@
             )
         return made
 
+    pl.semaphore_wait(barrier, sum(jnp.where(there, 1, 0) for there in exists))
+    land_copy = pltpu.make_async_remote_copy(
+        src_ref=land_ref.at[2 * (1 - parity)],
+        dst_ref=land.at[3],
+        send_sem=pair_send.at[0],
+        recv_sem=pair_recv.at[0],
+        device_id=(partner,),
+        device_id_type=MESH,
+    )
+    land_copy.start()
+
     for load in loads + small:
         load.wait()
     parent = [parents_ref[i] % 4 for i in range(2)]
@@ -255,17 +267,6 @@
     edges = dot(split(jnp.concatenate(edges, axis=0), 1), columns_up).reshape(2, 3, 4, 8, SIDE)
     for c in range(3):
         t0[c] = jnp.concatenate([edges[0, c], edges[1, c]], axis=0)
-
-    pl.semaphore_wait(barrier, sum(jnp.where(there, 1, 0) for there in exists))
-    land_copy = pltpu.make_async_remote_copy(
-        src_ref=land_ref.at[2 * (1 - parity)],
-        dst_ref=land.at[3],
-        send_sem=pair_send.at[0],
-        recv_sem=pair_recv.at[0],
-        device_id=(partner,),
-        device_id_type=MESH,
-    )
-    land_copy.start()
 
     for i in range(2):
         for c in range(3):
@@ -343,8 +344,6 @@
 
     strip = (8, 8, SIDE)
     sub = iota(strip, 1)
-    lane = iota(strip, 2)
-    sub_half = iota((8, 8, HALF), 1)
     lane_half = iota((8, 8, HALF), 2)
 
     def gather_outer():
@@ -383,19 +382,23 @@
         d, g = look_up(jnp.concatenate(classes, axis=0), tables)
         d, g = d.reshape(8, 2, 8, HALF), g.reshape(8, 2, 8, HALF)
         for c in range(3):
-            h0[c, :, :, HALF : HALF + SIDE] = walls[:, c]
+            h0[c, :, :, 0:SIDE] = walls[:, c]
         for j in range(2):
-            at = slice(HALF + j * HALF, 2 * HALF + j * HALF)
+            at = slice(j * HALF, HALF + j * HALF)
             outer_diffus[:, :, at] = d[:, j]
             outer_growth[:, :, at] = g[:, j]
 
+        low_half = lane8 < HALF // 2
         for i in range(2):
             for f in range(4):
                 pf = 4 * i + f
                 kind = f // 2
+                start = cross(2 * me + i, f)
+                chains = []
                 for e in range(2):
-                    patch, wall = cross(2 * me + i, f)
+                    patch, wall = start
                     side = 2 * (1 - kind) + e
+                    chain = []
                     for step in range(3):
                         if step % 2 == 0:
                             patch, side = cross(patch, side)
@@ -406,71 +409,71 @@
                         window = jnp.clip((patch >> 1) - me + REACH, 0, 2 * REACH)
                         row = corner_data[window, pl.ds(2 * (patch & 1) + x, 1), :]
                         row = jnp.broadcast_to(row, (8, HALF))
-                        row = jnp.where(y == 1, pltpu.roll(row, 64, 1), row)
-                        for q in range(5 if step < 2 else 3):
+                        chain.append(jnp.where(y == 1, pltpu.roll(row, 64, 1), row))
+                    chains.append(chain)
+                for step in range(3):
+                    for q in range(5 if step < 2 else 3):
+                        tiles = []
+                        for e in range(2):
                             if step < 2:
-                                tile = pick_lanes(row, index[kind, e] + 9 * q)
+                                at = index[kind, e] + 9 * q
                             else:
-                                tile = pick_lanes(row, jnp.full((8, HALF), 9 * q, jnp.int32))
-                            near = slice(3 * HALF * e, 3 * HALF * e + HALF)
-                            far = slice(HALF * e, HALF * e + HALF)
-                            if step == 0 and q < 3:
-                                h0[q, pf, :, near] = tile
-                            elif step == 0:
-                                (outer_diffus, outer_growth)[q - 3][pf, :, near] = tile
-                            elif step == 1 and q < 3:
-                                l0[q, pf, :, far] = tile
-                            elif step == 1:
-                                (far_diffus, far_growth)[q - 3][pf, :, far] = tile
-                            else:
-                                k0[q, pf, :, far] = tile
+                                at = jnp.full((8, HALF), 9 * q, jnp.int32)
+                            tiles.append(pick_lanes(chains[e][step], at))
+                        if step < 2:
+                            tile = jnp.where(low_half, tiles[1], tiles[0])
+                        else:
+                            tile = jnp.where(low_half, tiles[0], tiles[1])
+                        if step == 0 and q < 3:
+                            h0[q, pf, :, SIDE:] = tile
+                        elif step == 0:
+                            (outer_diffus, outer_growth)[q - 3][pf, :, SIDE:] = tile
+                        elif step == 1 and q < 3:
+                            l0[q, pf] = tile
+                        elif step == 1:
+                            (far_diffus, far_growth)[q - 3][pf] = tile
+                        else:
+                            k0[q, pf] = tile
 
     def rates_of(s, now, laps, diffus, growth):
         return scaled_rates(WEIGHTS[s], *now, *laps, diffus, growth)
 
+    rising = iota((8, HALF), 0)
+    falling = HALF - 1 - rising
+
     def strip_laplacian(now, beyond):
         ghost = jnp.broadcast_to(beyond[:, 0:1, :], strip)
-        low = jnp.sum(
-            jnp.where(lane_half == sub_half, ghost[:, :, :HALF], 0.0), axis=2, keepdims=True
-        )
-        high = jnp.sum(
-            jnp.where(lane_half == HALF - 1 - sub_half, ghost[:, :, HALF:], 0.0),
-            axis=2,
-            keepdims=True,
-        )
         ends = []
         for e in range(2):
             columns = []
             for i in range(2):
                 for f in range(4):
-                    face = 4 * i + (2 if f < 2 else 0) + e
-                    columns.append((low, high)[f % 2][face])
+                    face = ghost[4 * i + (2 if f < 2 else 0) + e]
+                    if f % 2:
+                        columns.append(pick_lanes(face[:, HALF:], falling))
+                    else:
+                        columns.append(pick_lanes(face[:, :HALF], rising))
             ends.append(jnp.stack(columns, axis=0))
         above = jnp.where(sub == 0, ghost, pltpu.roll(now, 1, 1))
         below = pltpu.roll(now, 7, 1)
-        left = jnp.where(lane == 0, ends[0], pltpu.roll(now, 1, 2))
-        right = jnp.where(lane == SIDE - 1, ends[1], pltpu.roll(now, SIDE - 1, 2))
+        rolled = pltpu.roll(now, 1, 2)
+        left = jnp.where(lane_half == 0, ends[0], rolled[:, :, :HALF])
+        left = jnp.concatenate([left, rolled[:, :, HALF:]], axis=2)
+        rolled = pltpu.roll(now, SIDE - 1, 2)
+        right = jnp.where(lane_half == HALF - 1, ends[1], rolled[:, :, HALF:])
+        right = jnp.concatenate([rolled[:, :, :HALF], right], axis=2)
         return (left + right) + (below + above) - 4.0 * now
 
-    wide = (8, 8, 2 * SIDE)
-
-    def wide_laplacian(now, facing):
-        above = jnp.where(iota(wide, 1) == 0, facing, pltpu.roll(now, 1, 1))
+    def round_laplacian(now, facing):
+        lanes = now.shape[2]
+        above = jnp.where(iota(now.shape, 1) == 0, facing, pltpu.roll(now, 1, 1))
         below = pltpu.roll(now, 7, 1)
-        sides = pltpu.roll(now, 1, 2) + pltpu.roll(now, 2 * SIDE - 1, 2)
+        sides = pltpu.roll(now, 1, 2) + pltpu.roll(now, lanes - 1, 2)
         return sides + (below + above) - 4.0 * now
-
-    def two_ends(block):
-        return jnp.concatenate([block[:, :, :HALF], block[:, :, HALF + SIDE :]], axis=2)
-
-    def between(ends, middle):
-        return jnp.concatenate([ends[:, :, :HALF], middle, ends[:, :, HALF:]], axis=2)
-
-    middle = slice(HALF, HALF + SIDE)
 
     def strip_stage(s):
         inner = [strips[s][c] for c in range(3)]
-        beyond = [outer[s][c, :, :, middle] for c in range(3)]
+        beyond = [outer[s][c, :, :, 0:SIDE] for c in range(3)]
         laps = [strip_laplacian(inner[c], beyond[c]) for c in range(3)]
         rates = rates_of(s, inner, laps, strip_diffus[...], strip_growth[...])
         if s == 3:
@@ -485,32 +488,33 @@
         for c in range(3):
             strips[s + 1][c] = t0[c] + rates[c]
         if s == 2:
-            now = beyond
             laps = []
             for c in range(3):
                 whole = outer[s][c]
-                above = jnp.where(sub == 0, inner[c], pltpu.roll(now[c], 1, 1))
-                sides = pltpu.roll(whole, 1, 2) + pltpu.roll(whole, 2 * SIDE - 1, 2)
-                laps.append(
-                    sides[:, :, middle] + (pltpu.roll(now[c], 7, 1) + above) - 4.0 * now[c]
-                )
+                now = beyond[c]
+                above = jnp.where(sub == 0, inner[c], pltpu.roll(now, 1, 1))
+                sides = pltpu.roll(whole, 1, 2) + pltpu.roll(whole, SIDE + HALF - 1, 2)
+                laps.append(sides[:, :, 0:SIDE] + (pltpu.roll(now, 7, 1) + above) - 4.0 * now)
             rates = rates_of(
-                s, now, laps, outer_diffus[:, :, middle], outer_growth[:, :, middle]
+                s, beyond, laps, outer_diffus[:, :, 0:SIDE], outer_growth[:, :, 0:SIDE]
             )
             for c in range(3):
-                outer[3][c, :, :, middle] = h0[c, :, :, middle] + rates[c]
+                outer[3][c, :, :, 0:SIDE] = h0[c, :, :, 0:SIDE] + rates[c]
             return
         far = [(l0, l1)[s][c] for c in range(3)]
         now = [outer[s][c] for c in range(3)]
-        laps = [wide_laplacian(now[c], between(far[c], inner[c])) for c in range(3)]
+        laps = [
+            round_laplacian(now[c], jnp.concatenate([inner[c], far[c]], axis=2)) for c in range(3)
+        ]
         rates = rates_of(s, now, laps, outer_diffus[...], outer_growth[...])
         for c in range(3):
             outer[s + 1][c] = h0[c] + rates[c]
         if s == 0:
             laps = []
             for c in range(3):
-                lap = wide_laplacian(between(far[c], k0[c]), now[c])
-                laps.append(two_ends(lap))
+                both = jnp.concatenate([far[c], k0[c]], axis=2)
+                facing = jnp.concatenate([now[c][:, :, SIDE:], k0[c]], axis=2)
+                laps.append(round_laplacian(both, facing)[:, :, :HALF])
             rates = rates_of(s, far, laps, far_diffus[...], far_growth[...])
             for c in range(3):
                 l1[c] = far[c] + rates[c]
@@ -583,16 +587,18 @@
 
     result_copy = to_partner(1, result, result_out)
     ring_copy = to_partner(2, ring, ring_out)
-    own_copies = []
-    for i in range(2):
-        own_copies.append(pltpu.make_async_copy(result.at[i], result_out.at[i], own_sem.at[i]))
-    own_copies.append(pltpu.make_async_copy(ring, ring_out.at[pl.ds(0, 2)], own_sem.at[2]))
-    for i in (moving, parity):
-        for s in range(4):
-            bulk_stage(i, s)
-        bulk_weave(i)
-        if i is moving:
-            result_copy.start()
+    own_copies = [
+        pltpu.make_async_copy(result.at[moving], result_out.at[moving], own_sem.at[0]),
+        pltpu.make_async_copy(ring, ring_out.at[pl.ds(0, 2)], own_sem.at[1]),
+        pltpu.make_async_copy(result.at[parity], result_out.at[parity], own_sem.at[2]),
+    ]
+    for s in range(4):
+        bulk_stage(moving, s)
+    bulk_weave(moving)
+    result_copy.start()
+    own_copies[0].start()
+    for s in range(2):
+        bulk_stage(parity, s)
     for n, copy in enumerate(face_copies()):
         pl.when(exists[n ^ 1])(copy.wait_recv)
     for n, copy in enumerate(corner_copies()):
@@ -601,8 +607,11 @@
     for s in range(4):
         strip_stage(s)
     ring_copy.start()
-    for copy in own_copies:
-        copy.start()
+    own_copies[1].start()
+    for s in range(2, 4):
+        bulk_stage(parity, s)
+    bulk_weave(parity)
+    own_copies[2].start()
     for n, copy in enumerate(face_copies()):
         pl.when(exists[n])(copy.wait_send)
     for n, copy in enumerate(corner_copies()):
@@ -716,7 +725,8 @@
     hbm = pl.BlockSpec(memory_space=pltpu.HBM)
     stage_buf = pltpu.VMEM((2, 3, 2, 2, HALF + 2 * PAD, HALF), f32)
     strip_buf = pltpu.VMEM((3, 8, 8, SIDE), f32)
-    outer_buf = pltpu.VMEM((3, 8, 8, 2 * SIDE), f32)
+    outer_buf = pltpu.VMEM((3, 8, 8, SIDE + HALF), f32)
+    far_buf = pltpu.VMEM((3, 8, 8, HALF), f32)
     results = jax.ShapeDtypeStruct((3, 3, 2, SIDE, HALF), f32)
     rings = jax.ShapeDtypeStruct((3, 3, 4, 8, SIDE), f32)
     whole, outer = pl.pallas_call(
@@ -752,13 +762,13 @@
             outer_buf,
             outer_buf,
             outer_buf,
-            pltpu.VMEM((8, 8, 2 * SIDE), f32),
-            pltpu.VMEM((8, 8, 2 * SIDE), f32),
-            strip_buf,
-            strip_buf,
-            pltpu.VMEM((8, 8, SIDE), f32),
-            pltpu.VMEM((8, 8, SIDE), f32),
-            strip_buf,
+            pltpu.VMEM((8, 8, SIDE + HALF), f32),
+            pltpu.VMEM((8, 8, SIDE + HALF), f32),
+            far_buf,
+            far_buf,
+            pltpu.VMEM((8, 8, HALF), f32),
+            pltpu.VMEM((8, 8, HALF), f32),
+            far_buf,
             pltpu.SemaphoreType.DMA((4,)),
             pltpu.SemaphoreType.DMA((5,)),
             pltpu.SemaphoreType.DMA,
@@ -771,7 +781,7 @@
             pltpu.SemaphoreType.DMA((3,)),
         ],
         compiler_params=pltpu.CompilerParams(
-            collective_id=0, has_side_effects=True, vmem_limit_bytes=62 * 1024 * 1024
+            collective_id=0, has_side_effects=True, vmem_limit_bytes=VMEM_LIMIT
         ),
         name="regrid_step",
     )(parents, new_counts, neighbours.T, class_diffusivity, class_growth, coarse, land_cover)
@@ -791,7 +801,7 @@
             pltpu.SemaphoreType.DMA((3, 3, 2)),
             pltpu.SemaphoreType.DMA((2,)),
         ],
-        compiler_params=pltpu.CompilerParams(vmem_limit_bytes=62 * 1024 * 1024),
+        compiler_params=pltpu.CompilerParams(vmem_limit_bytes=VMEM_LIMIT),
         name="merge_slots",
     )(new_counts, whole, outer)
 

time: 25.4 us -> 22.4 us (0.88)
  Pallas kernels: 25.2 us -> 22.2 us
    pallas_call x1, Pallas kernels: 22 us -> 19 us  [body(): pl.pallas_call(functools.partial(kernel, owners), out_shape=(results, rin...]
where the time goes in v4:
time: 22.4 us; the launch traced here: 22.2 us
  Pallas kernels  22.2 us (99%)
    pallas_call x1, Pallas kernels, body(): pl.pallas_call(functools.partial(kernel, owners), out_shape=(results, rin...  19 us
    pallas_call x1, Pallas kernels, body(): pl.pallas_call(merge_kernel, out_shape=jax.ShapeDtypeStruct((3, 3, SIDE,...  3.21 us

profile of v4, /device:TPU:25, one launch (start us, length us, event | category | flops | bytes accessed | tf_op | source)
XLA Modules:
  0.0 22.2 jit_solution(3983326363174287708)
XLA Ops:
  0.0 19.0 %regrid_step.1 = (f32[3,3,2,256,128]{4,3,2,1,0:T(8,128)}, f32[3,3,4,8,256]{4,3,2,1,0:T(8,128)}) custom-call(s32[2]{0:T(128)} %parents_hbm.1, s32[128]{0:T(128)} %counts_hbm.3, s32[4,256]{1,0:T(4,128)} %bitcast.1, f32[11]{0:T(128)} %diff_hbm.1, f32[11]{0:T(128)} %grow_hbm.1, f32[1,3,256,256]{3,2,1,0:T(8,128)} %coarse_ref.1, s32[3,256,256]{2,1,0:T(8,128)} %land_ref.1), custom_call_target="tpu_custom_call" | custom-call | tf_op jit(solution)/shard_map/regrid_step/pallas_call | solution.py:732
  19.0 3.2 %merge_slots.1 = f32[3,3,256,256]{3,2,1,0:T(8,128)} custom-call(s32[128]{0:T(128)} %counts_hbm.3, f32[3,3,2,256,128]{4,3,2,1,0:T(8,128)} %get-tuple-element.7.result_hbm, f32[3,3,4,8,256]{4,3,2,1,0:T(8,128)} %get-tuple-element.8.ring_hbm), custom_call_target="tpu_custom_call" | custom-call | tf_op jit(solution)/shard_map/merge_slots/pallas_call | solution.py:788

commit v5 on v4

--- a/solution.py
+++ b/solution.py
@@ -106,6 +106,7 @@
     grow_ref,
     quads,
     land,
+    land_far,
     x_buf,
     s2_buf,
     s3_buf,
@@ -172,7 +173,7 @@
     for n, (src, dst) in enumerate(pairs):
         small.append(pltpu.make_async_copy(src, dst, small_sem.at[n]))
         small[n].start()
-    land_load = pltpu.make_async_copy(land_ref, land.at[pl.ds(0, 3)], land_sem)
+    land_load = pltpu.make_async_copy(land_ref, land, land_sem)
     land_load.start()
     barrier = pltpu.get_barrier_semaphore()
     for n in range(len(steps)):
@@ -240,16 +241,49 @@
             )
         return made
 
-    pl.semaphore_wait(barrier, sum(jnp.where(there, 1, 0) for there in exists))
-    land_copy = pltpu.make_async_remote_copy(
-        src_ref=land_ref.at[2 * (1 - parity)],
-        dst_ref=land.at[3],
-        send_sem=pair_send.at[0],
-        recv_sem=pair_recv.at[0],
-        device_id=(partner,),
-        device_id_type=MESH,
-    )
-    land_copy.start()
+    def bulk_stage(i, s):
+        src = stages[s]
+        dst = stages[(s + 1) % 4] if s < 3 else s2_buf
+
+        def step_rows(step, carry):
+            r = pl.multiple_of(step * 8, 8)
+            at = PAD + r
+            here = pl.ds(at, 8)
+            now = [[src[i, c, n // 2, n % 2, here, :] for n in range(4)] for c in range(3)]
+            lap = [[None] * 4 for _ in range(3)]
+            for c in range(3):
+                for n in range(4):
+                    y, x = n // 2, n % 2
+                    beside = now[c][2 * y + 1 - x]
+                    beyond = pltpu.roll(beside, HALF - 1 if x else 1, 1)
+                    upright = now[c][2 * (1 - y) + x]
+                    further = src[i, c, 1 - y, x, pl.ds(at + 2 * y - 1, 8), :]
+                    lap[c][n] = (beside + beyond) + (upright + further) - 4.0 * now[c][n]
+            for n in range(4):
+                y, x = n // 2, n % 2
+                rates = scaled_rates(
+                    WEIGHTS[s],
+                    *[now[c][n] for c in range(3)],
+                    *[lap[c][n] for c in range(3)],
+                    diffus_buf[i, y, x, pl.ds(r, 8), :],
+                    growth_buf[i, y, x, pl.ds(r, 8), :],
+                )
+                for c in range(3):
+                    base = now[c][n] if s == 0 else x_buf[i, c, y, x, here, :]
+                    if s < 3:
+                        value = base + rates[c]
+                    else:
+                        value = combine(
+                            base,
+                            s2_buf[i, c, y, x, here, :],
+                            s3_buf[i, c, y, x, here, :],
+                            now[c][n],
+                            rates[c],
+                        )
+                    dst[i, c, y, x, here, :] = value
+            return carry
+
+        lax.fori_loop(0, HALF // 8, step_rows, 0, unroll=4)
 
     for load in loads + small:
         load.wait()
@@ -278,19 +312,21 @@
                         y * HALF : (y + 1) * HALF, x * HALF : (x + 1) * HALF
                     ]
 
-    land_load.wait()
-    land_copy.wait_recv()
+    pl.semaphore_wait(barrier, sum(jnp.where(there, 1, 0) for there in exists))
+    land_copy = pltpu.make_async_remote_copy(
+        src_ref=land_ref.at[2 * (1 - parity)],
+        dst_ref=land_far,
+        send_sem=pair_send.at[0],
+        recv_sem=pair_recv.at[0],
+        device_id=(partner,),
+        device_id_type=MESH,
+    )
+    land_copy.start()
+
     count = counts_ref[me]
-    slots = []
-    for i in range(2):
-        even_slot = jnp.where(i >= count, 3, i)
-        odd_slot = jnp.where(i - 2 + count < 0, 3, i - 2 + count)
-        slots.append(jnp.where(parity == 0, even_slot, odd_slot))
     tables = (table_of(diff_ref), table_of(grow_ref))
-    classes_of = []
-    for i in range(2):
-        classes = land[slots[i]].astype(jnp.float32).astype(jnp.bfloat16)
-        classes_of.append(classes)
+
+    def rim_rates(i, classes):
         rims = jnp.concatenate([dot_t(edge_pick, classes), dot(edge_pick, classes)], axis=0)
         d, g = look_up(rims, tables)
         for f in range(4):
@@ -304,6 +340,30 @@
                     face_data[3 + i, f, at : at + 1, :] = rims[
                         row : row + 1, j * HALF : (j + 1) * HALF
                     ]
+
+    def bulk_rates(i, classes):
+        classes = dot(classes, unweave).astype(jnp.bfloat16)
+        for n in range(8):
+            rows = slice(32 * n, 32 * n + 32)
+            d, g = look_up(dot(weave[rows], classes), tables)
+            y, m = n // 4, 32 * (n % 4)
+            for x in range(2):
+                diffus_buf[i, y, x, m : m + 32] = d[:, x * HALF : (x + 1) * HALF]
+                growth_buf[i, y, x, m : m + 32] = g[:, x * HALF : (x + 1) * HALF]
+
+    land_load.wait()
+    classes = land[jnp.where(parity == 0, 0, jnp.clip(count - 1, 0, 2))]
+    classes = classes.astype(jnp.float32).astype(jnp.bfloat16)
+    rim_rates(parity, classes)
+    bulk_rates(parity, classes)
+    bulk_stage(parity, 0)
+
+    land_copy.wait_recv()
+    classes = jnp.where(
+        count < 2, land_far[...], land[jnp.where(parity == 0, 1, jnp.clip(count - 2, 0, 2))]
+    )
+    classes = classes.astype(jnp.float32).astype(jnp.bfloat16)
+    rim_rates(moving, classes)
 
     lane8, sub8 = iota((8, HALF), 1), iota((8, HALF), 0)
     for i in range(2):
@@ -327,15 +387,7 @@
     for n, copy in enumerate(corner_copies()):
         pl.when(exists[n])(copy.start)
 
-    for i in range(2):
-        classes = dot(classes_of[i], unweave).astype(jnp.bfloat16)
-        for n in range(8):
-            rows = slice(32 * n, 32 * n + 32)
-            d, g = look_up(dot(weave[rows], classes), tables)
-            y, m = n // 4, 32 * (n % 4)
-            for x in range(2):
-                diffus_buf[i, y, x, m : m + 32] = d[:, x * HALF : (x + 1) * HALF]
-                growth_buf[i, y, x, m : m + 32] = g[:, x * HALF : (x + 1) * HALF]
+    bulk_rates(moving, classes)
 
     def cross(patch, face):
         value = nb_ref[face, patch]
@@ -519,50 +571,6 @@
             for c in range(3):
                 l1[c] = far[c] + rates[c]
 
-    def bulk_stage(i, s):
-        src = stages[s]
-        dst = stages[(s + 1) % 4] if s < 3 else s2_buf
-
-        def step_rows(step, carry):
-            r = pl.multiple_of(step * 8, 8)
-            at = PAD + r
-            here = pl.ds(at, 8)
-            now = [[src[i, c, n // 2, n % 2, here, :] for n in range(4)] for c in range(3)]
-            lap = [[None] * 4 for _ in range(3)]
-            for c in range(3):
-                for n in range(4):
-                    y, x = n // 2, n % 2
-                    beside = now[c][2 * y + 1 - x]
-                    beyond = pltpu.roll(beside, HALF - 1 if x else 1, 1)
-                    upright = now[c][2 * (1 - y) + x]
-                    further = src[i, c, 1 - y, x, pl.ds(at + 2 * y - 1, 8), :]
-                    lap[c][n] = (beside + beyond) + (upright + further) - 4.0 * now[c][n]
-            for n in range(4):
-                y, x = n // 2, n % 2
-                rates = scaled_rates(
-                    WEIGHTS[s],
-                    *[now[c][n] for c in range(3)],
-                    *[lap[c][n] for c in range(3)],
-                    diffus_buf[i, y, x, pl.ds(r, 8), :],
-                    growth_buf[i, y, x, pl.ds(r, 8), :],
-                )
-                for c in range(3):
-                    base = now[c][n] if s == 0 else x_buf[i, c, y, x, here, :]
-                    if s < 3:
-                        value = base + rates[c]
-                    else:
-                        value = combine(
-                            base,
-                            s2_buf[i, c, y, x, here, :],
-                            s3_buf[i, c, y, x, here, :],
-                            now[c][n],
-                            rates[c],
-                        )
-                    dst[i, c, y, x, here, :] = value
-            return carry
-
-        lax.fori_loop(0, HALF // 8, step_rows, 0, unroll=4)
-
     def bulk_weave(i):
         for c in range(3):
             for y in range(2):
@@ -597,8 +605,7 @@
     bulk_weave(moving)
     result_copy.start()
     own_copies[0].start()
-    for s in range(2):
-        bulk_stage(parity, s)
+    bulk_stage(parity, 1)
     for n, copy in enumerate(face_copies()):
         pl.when(exists[n ^ 1])(copy.wait_recv)
     for n, copy in enumerate(corner_copies()):
@@ -741,7 +748,8 @@
             pltpu.SMEM((CLASSES,), f32),
             pltpu.SMEM((CLASSES,), f32),
             pltpu.VMEM((4, 3, HALF, HALF), f32),
-            pltpu.VMEM((4, SIDE, SIDE), jnp.int32),
+            pltpu.VMEM((3, SIDE, SIDE), jnp.int32),
+            pltpu.VMEM((SIDE, SIDE), jnp.int32),
             stage_buf,
             stage_buf,
             stage_buf,

time: 22.4 us -> 23.2 us (1.036)
  Pallas kernels: 22.2 us -> 23.1 us
    pallas_call x1, Pallas kernels: 19 us -> 19.6 us  [body(): pl.pallas_call(functools.partial(kernel, owners), out_shape=(results, rin...]
    pallas_call x1, Pallas kernels: 3.21 us -> 3.5 us  [body(): pl.pallas_call(merge_kernel, out_shape=jax.ShapeDtypeStruct((3, 3, SIDE,...]
where the time goes in v5:
time: 23.2 us; the launch traced here: 23.1 us
  Pallas kernels  23.1 us (100%)
    pallas_call x1, Pallas kernels, body(): pl.pallas_call(functools.partial(kernel, owners), out_shape=(results, rin...  19.6 us
    pallas_call x1, Pallas kernels, body(): pl.pallas_call(merge_kernel, out_shape=jax.ShapeDtypeStruct((3, 3, SIDE,...  3.5 us

profile of v5, /device:TPU:25, one launch (start us, length us, event | category | flops | bytes accessed | tf_op | source)
XLA Modules:
  0.0 23.1 jit_solution(9568625956278351667)
XLA Ops:
  0.0 19.6 %regrid_step.1 = (f32[3,3,2,256,128]{4,3,2,1,0:T(8,128)}, f32[3,3,4,8,256]{4,3,2,1,0:T(8,128)}) custom-call(s32[2]{0:T(128)} %parents_hbm.1, s32[128]{0:T(128)} %counts_hbm.3, s32[4,256]{1,0:T(4,128)} %bitcast.1, f32[11]{0:T(128)} %diff_hbm.1, f32[11]{0:T(128)} %grow_hbm.1, f32[1,3,256,256]{3,2,1,0:T(8,128)} %coarse_ref.1, s32[3,256,256]{2,1,0:T(8,128)} %land_ref.1), custom_call_target="tpu_custom_call" | custom-call | tf_op jit(solution)/shard_map/regrid_step/pallas_call | solution.py:739
  19.6 3.5 %merge_slots.1 = f32[3,3,256,256]{3,2,1,0:T(8,128)} custom-call(s32[128]{0:T(128)} %counts_hbm.3, f32[3,3,2,256,128]{4,3,2,1,0:T(8,128)} %get-tuple-element.7.result_hbm, f32[3,3,4,8,256]{4,3,2,1,0:T(8,128)} %get-tuple-element.8.ring_hbm), custom_call_target="tpu_custom_call" | custom-call | tf_op jit(solution)/shard_map/merge_slots/pallas_call | solution.py:796

commit v6 on v4

--- a/solution.py
+++ b/solution.py
@@ -561,7 +561,7 @@
                     dst[i, c, y, x, here, :] = value
             return carry
 
-        lax.fori_loop(0, HALF // 8, step_rows, 0, unroll=4)
+        lax.fori_loop(0, HALF // 8, step_rows, 0, unroll=8)
 
     def bulk_weave(i):
         for c in range(3):
@@ -597,7 +597,7 @@
     bulk_weave(moving)
     result_copy.start()
     own_copies[0].start()
-    for s in range(2):
+    for s in range(4):
         bulk_stage(parity, s)
     for n, copy in enumerate(face_copies()):
         pl.when(exists[n ^ 1])(copy.wait_recv)
@@ -608,8 +608,6 @@
         strip_stage(s)
     ring_copy.start()
     own_copies[1].start()
-    for s in range(2, 4):
-        bulk_stage(parity, s)
     bulk_weave(parity)
     own_copies[2].start()
     for n, copy in enumerate(face_copies()):

time: 22.4 us -> 21.4 us (0.955)
  Pallas kernels: 22.2 us -> 21.3 us
    pallas_call x1, Pallas kernels: 19 us -> 18.1 us  [body(): pl.pallas_call(functools.partial(kernel, owners), out_shape=(results, rin...]
where the time goes in v6:
time: 21.4 us; the launch traced here: 21.3 us
  Pallas kernels  21.3 us (100%)
    pallas_call x1, Pallas kernels, body(): pl.pallas_call(functools.partial(kernel, owners), out_shape=(results, rin...  18.1 us
    pallas_call x1, Pallas kernels, body(): pl.pallas_call(merge_kernel, out_shape=jax.ShapeDtypeStruct((3, 3, SIDE,...  3.21 us

profile of v6, /device:TPU:25, one launch (start us, length us, event | category | flops | bytes accessed | tf_op | source)
XLA Modules:
  0.0 21.3 jit_solution(6150397999782083997)
XLA Ops:
  0.0 18.1 %regrid_step.1 = (f32[3,3,2,256,128]{4,3,2,1,0:T(8,128)}, f32[3,3,4,8,256]{4,3,2,1,0:T(8,128)}) custom-call(s32[2]{0:T(128)} %parents_hbm.1, s32[128]{0:T(128)} %counts_hbm.3, s32[4,256]{1,0:T(4,128)} %bitcast.1, f32[11]{0:T(128)} %diff_hbm.1, f32[11]{0:T(128)} %grow_hbm.1, f32[1,3,256,256]{3,2,1,0:T(8,128)} %coarse_ref.1, s32[3,256,256]{2,1,0:T(8,128)} %land_ref.1), custom_call_target="tpu_custom_call" | custom-call | tf_op jit(solution)/shard_map/regrid_step/pallas_call | solution.py:730
  18.1 3.2 %merge_slots.1 = f32[3,3,256,256]{3,2,1,0:T(8,128)} custom-call(s32[128]{0:T(128)} %counts_hbm.3, f32[3,3,2,256,128]{4,3,2,1,0:T(8,128)} %get-tuple-element.7.result_hbm, f32[3,3,4,8,256]{4,3,2,1,0:T(8,128)} %get-tuple-element.8.ring_hbm), custom_call_target="tpu_custom_call" | custom-call | tf_op jit(solution)/shard_map/merge_slots/pallas_call | solution.py:786

commit v7 on v6

--- a/solution.py
+++ b/solution.py
@@ -561,7 +561,7 @@
                     dst[i, c, y, x, here, :] = value
             return carry
 
-        lax.fori_loop(0, HALF // 8, step_rows, 0, unroll=8)
+        lax.fori_loop(0, HALF // 8, step_rows, 0, unroll=16)
 
     def bulk_weave(i):
         for c in range(3):

time: 21.4 us -> 20.8 us (0.972)
  Pallas kernels: 21.3 us -> 20.7 us
    pallas_call x1, Pallas kernels: 18.1 us -> 17.5 us  [body(): pl.pallas_call(functools.partial(kernel, owners), out_shape=(results, rin...]
where the time goes in v7:
time: 20.8 us; the launch traced here: 20.7 us
  Pallas kernels  20.7 us (100%)
    pallas_call x1, Pallas kernels, body(): pl.pallas_call(functools.partial(kernel, owners), out_shape=(results, rin...  17.5 us
    pallas_call x1, Pallas kernels, body(): pl.pallas_call(merge_kernel, out_shape=jax.ShapeDtypeStruct((3, 3, SIDE,...  3.21 us

profile of v7, /device:TPU:25, one launch (start us, length us, event | category | flops | bytes accessed | tf_op | source)
XLA Modules:
  0.0 20.7 jit_solution(569766908006865101)
XLA Ops:
  0.0 17.5 %regrid_step.1 = (f32[3,3,2,256,128]{4,3,2,1,0:T(8,128)}, f32[3,3,4,8,256]{4,3,2,1,0:T(8,128)}) custom-call(s32[2]{0:T(128)} %parents_hbm.1, s32[128]{0:T(128)} %counts_hbm.3, s32[4,256]{1,0:T(4,128)} %bitcast.1, f32[11]{0:T(128)} %diff_hbm.1, f32[11]{0:T(128)} %grow_hbm.1, f32[1,3,256,256]{3,2,1,0:T(8,128)} %coarse_ref.1, s32[3,256,256]{2,1,0:T(8,128)} %land_ref.1), custom_call_target="tpu_custom_call" | custom-call | tf_op jit(solution)/shard_map/regrid_step/pallas_call | solution.py:730
  17.5 3.2 %merge_slots.1 = f32[3,3,256,256]{3,2,1,0:T(8,128)} custom-call(s32[128]{0:T(128)} %counts_hbm.3, f32[3,3,2,256,128]{4,3,2,1,0:T(8,128)} %get-tuple-element.7.result_hbm, f32[3,3,4,8,256]{4,3,2,1,0:T(8,128)} %get-tuple-element.8.ring_hbm), custom_call_target="tpu_custom_call" | custom-call | tf_op jit(solution)/shard_map/merge_slots/pallas_call | solution.py:786

commit v8 on v5

--- a/solution.py
+++ b/solution.py
@@ -283,7 +283,7 @@
                     dst[i, c, y, x, here, :] = value
             return carry
 
-        lax.fori_loop(0, HALF // 8, step_rows, 0, unroll=4)
+        lax.fori_loop(0, HALF // 8, step_rows, 0, unroll=8)
 
     for load in loads + small:
         load.wait()
@@ -605,7 +605,8 @@
     bulk_weave(moving)
     result_copy.start()
     own_copies[0].start()
-    bulk_stage(parity, 1)
+    for s in range(1, 4):
+        bulk_stage(parity, s)
     for n, copy in enumerate(face_copies()):
         pl.when(exists[n ^ 1])(copy.wait_recv)
     for n, copy in enumerate(corner_copies()):
@@ -615,8 +616,6 @@
         strip_stage(s)
     ring_copy.start()
     own_copies[1].start()
-    for s in range(2, 4):
-        bulk_stage(parity, s)
     bulk_weave(parity)
     own_copies[2].start()
     for n, copy in enumerate(face_copies()):

time: 23.2 us -> 21.9 us (0.944)
  Pallas kernels: 23.1 us -> 21.8 us
    pallas_call x1, Pallas kernels: 19.6 us -> 18.5 us  [body(): pl.pallas_call(functools.partial(kernel, owners), out_shape=(results, rin...]
    pallas_call x1, Pallas kernels: 3.5 us -> 3.21 us  [body(): pl.pallas_call(merge_kernel, out_shape=jax.ShapeDtypeStruct((3, 3, SIDE,...]
where the time goes in v8:
time: 21.9 us; the launch traced here: 21.8 us
  Pallas kernels  21.8 us (100%)
    pallas_call x1, Pallas kernels, body(): pl.pallas_call(functools.partial(kernel, owners), out_shape=(results, rin...  18.5 us
    pallas_call x1, Pallas kernels, body(): pl.pallas_call(merge_kernel, out_shape=jax.ShapeDtypeStruct((3, 3, SIDE,...  3.21 us

profile of v8, /device:TPU:25, one launch (start us, length us, event | category | flops | bytes accessed | tf_op | source)
XLA Modules:
  0.0 21.8 jit_solution(9612887844129944097)
XLA Ops:
  0.0 18.5 %regrid_step.1 = (f32[3,3,2,256,128]{4,3,2,1,0:T(8,128)}, f32[3,3,4,8,256]{4,3,2,1,0:T(8,128)}) custom-call(s32[2]{0:T(128)} %parents_hbm.1, s32[128]{0:T(128)} %counts_hbm.3, s32[4,256]{1,0:T(4,128)} %bitcast.1, f32[11]{0:T(128)} %diff_hbm.1, f32[11]{0:T(128)} %grow_hbm.1, f32[1,3,256,256]{3,2,1,0:T(8,128)} %coarse_ref.1, s32[3,256,256]{2,1,0:T(8,128)} %land_ref.1), custom_call_target="tpu_custom_call" | custom-call | tf_op jit(solution)/shard_map/regrid_step/pallas_call | solution.py:738
  18.5 3.2 %merge_slots.1 = f32[3,3,256,256]{3,2,1,0:T(8,128)} custom-call(s32[128]{0:T(128)} %counts_hbm.3, f32[3,3,2,256,128]{4,3,2,1,0:T(8,128)} %get-tuple-element.7.result_hbm, f32[3,3,4,8,256]{4,3,2,1,0:T(8,128)} %get-tuple-element.8.ring_hbm), custom_call_target="tpu_custom_call" | custom-call | tf_op jit(solution)/shard_map/merge_slots/pallas_call | solution.py:795

commit v9 on v6

--- a/solution.py
+++ b/solution.py
@@ -599,6 +599,8 @@
     own_copies[0].start()
     for s in range(4):
         bulk_stage(parity, s)
+    bulk_weave(parity)
+    own_copies[2].start()
     for n, copy in enumerate(face_copies()):
         pl.when(exists[n ^ 1])(copy.wait_recv)
     for n, copy in enumerate(corner_copies()):
@@ -608,8 +610,6 @@
         strip_stage(s)
     ring_copy.start()
     own_copies[1].start()
-    bulk_weave(parity)
-    own_copies[2].start()
     for n, copy in enumerate(face_copies()):
         pl.when(exists[n])(copy.wait_send)
     for n, copy in enumerate(corner_copies()):

time: 21.4 us -> 21.9 us (1.023)
  Pallas kernels: 21.3 us -> 21.8 us
    pallas_call x1, Pallas kernels: 3.21 us -> 3.5 us  [body(): pl.pallas_call(merge_kernel, out_shape=jax.ShapeDtypeStruct((3, 3, SIDE,...]
where the time goes in v9:
time: 21.9 us; the launch traced here: 21.8 us
  Pallas kernels  21.8 us (100%)
    pallas_call x1, Pallas kernels, body(): pl.pallas_call(functools.partial(kernel, owners), out_shape=(results, rin...  18.3 us
    pallas_call x1, Pallas kernels, body(): pl.pallas_call(merge_kernel, out_shape=jax.ShapeDtypeStruct((3, 3, SIDE,...  3.5 us

profile of v9, /device:TPU:25, one launch (start us, length us, event | category | flops | bytes accessed | tf_op | source)
XLA Modules:
  0.0 21.8 jit_solution(13766948400811844385)
XLA Ops:
  0.0 18.3 %regrid_step.1 = (f32[3,3,2,256,128]{4,3,2,1,0:T(8,128)}, f32[3,3,4,8,256]{4,3,2,1,0:T(8,128)}) custom-call(s32[2]{0:T(128)} %parents_hbm.1, s32[128]{0:T(128)} %counts_hbm.3, s32[4,256]{1,0:T(4,128)} %bitcast.1, f32[11]{0:T(128)} %diff_hbm.1, f32[11]{0:T(128)} %grow_hbm.1, f32[1,3,256,256]{3,2,1,0:T(8,128)} %coarse_ref.1, s32[3,256,256]{2,1,0:T(8,128)} %land_ref.1), custom_call_target="tpu_custom_call" | custom-call | tf_op jit(solution)/shard_map/regrid_step/pallas_call | solution.py:730
  18.3 3.5 %merge_slots.1 = f32[3,3,256,256]{3,2,1,0:T(8,128)} custom-call(s32[128]{0:T(128)} %counts_hbm.3, f32[3,3,2,256,128]{4,3,2,1,0:T(8,128)} %get-tuple-element.7.result_hbm, f32[3,3,4,8,256]{4,3,2,1,0:T(8,128)} %get-tuple-element.8.ring_hbm), custom_call_target="tpu_custom_call" | custom-call | tf_op jit(solution)/shard_map/merge_slots/pallas_call | solution.py:786

commit v10 on v7

--- a/solution.py
+++ b/solution.py
@@ -120,7 +120,8 @@
     t3,
     strip_diffus,
     strip_growth,
-    face_data,
+    wall_data,
+    class_data,
     corner_data,
     h0,
     h1,
@@ -204,12 +205,13 @@
                         buf[i, c, y, x, 0:PAD] = jnp.zeros((PAD, HALF), jnp.float32)
                         buf[i, c, y, x, PAD + HALF :] = jnp.zeros((PAD, HALF), jnp.float32)
 
-    def face_copies():
+    def face_copies(k):
+        data = (wall_data, class_data)[k]
         ends = [
-            (face_data.at[pl.ds(3, 2)], face_data.at[pl.ds(1, 2)]),
-            (face_data.at[pl.ds(3, 2)], face_data.at[pl.ds(5, 2)]),
-            (face_data.at[4], face_data.at[0]),
-            (face_data.at[3], face_data.at[7]),
+            (data.at[pl.ds(3, 2)], data.at[pl.ds(1, 2)]),
+            (data.at[pl.ds(3, 2)], data.at[pl.ds(5, 2)]),
+            (data.at[4], data.at[0]),
+            (data.at[3], data.at[7]),
         ]
         made = []
         for n, (src, dst) in enumerate(ends):
@@ -217,8 +219,8 @@
                 pltpu.make_async_remote_copy(
                     src_ref=src,
                     dst_ref=dst,
-                    send_sem=face_send.at[n],
-                    recv_sem=face_recv.at[n],
+                    send_sem=face_send.at[k, n],
+                    recv_sem=face_recv.at[k, n],
                     device_id=(reach[n],),
                     device_id_type=MESH,
                 )
@@ -263,7 +265,9 @@
             edges += [across[0:16], along[0:16]]
             for f in range(4):
                 rows = (across, along)[f // 2][16 + 8 * (f % 2) : 19 + 8 * (f % 2)]
-                face_data[3 + i, f, 3 * c : 3 * c + 3, :] = rows
+                wall_data[3 + i, 9 * f + 3 * c : 9 * f + 3 * c + 3, :] = rows
+    for n, copy in enumerate(face_copies(0)):
+        pl.when(exists[n])(copy.start)
     edges = dot(split(jnp.concatenate(edges, axis=0), 1), columns_up).reshape(2, 3, 4, 8, SIDE)
     for c in range(3):
         t0[c] = jnp.concatenate([edges[0, c], edges[1, c]], axis=0)
@@ -299,9 +303,9 @@
             strip_growth[4 * i + f] = g[rows]
             for a in range(3):
                 for j in range(2):
-                    at = 9 + 2 * a + j
+                    at = 6 * f + 2 * a + j
                     row = 8 * f + a
-                    face_data[3 + i, f, at : at + 1, :] = rims[
+                    class_data[3 + i, at : at + 1, :] = rims[
                         row : row + 1, j * HALF : (j + 1) * HALF
                     ]
 
@@ -322,7 +326,7 @@
             at = 2 * i + x
             corner_data[REACH, at : at + 1, :] = jnp.sum(row, axis=0, keepdims=True)
 
-    for n, copy in enumerate(face_copies()):
+    for n, copy in enumerate(face_copies(1)):
         pl.when(exists[n])(copy.start)
     for n, copy in enumerate(corner_copies()):
         pl.when(exists[n])(copy.start)
@@ -366,17 +370,14 @@
                 for c in range(3):
                     parts = []
                     for a in range(3):
-                        at = 3 * c + a
-                        row = face_data[where, face, at : at + 1, :]
+                        row = wall_data[where, pl.ds(9 * face + 3 * c + a, 1), :]
                         parts.append(first[a] * jnp.broadcast_to(row, (8, HALF)))
                     walls.append(parts[0] + parts[1] + parts[2])
                 for j in range(2):
                     rows = []
                     for a in range(3):
-                        at = 9 + 2 * a + j
-                        rows.append(
-                            jnp.broadcast_to(face_data[where, face, at : at + 1, :], (8, HALF))
-                        )
+                        row = class_data[where, pl.ds(6 * face + 2 * a + j, 1), :]
+                        rows.append(jnp.broadcast_to(row, (8, HALF)))
                     classes.append(jnp.where(sub8 == 0, rows[0], jnp.where(sub8 == 1, rows[1], rows[2])))
         walls = dot(split(jnp.concatenate(walls, axis=0), 1), columns_up).reshape(8, 3, 8, SIDE)
         d, g = look_up(jnp.concatenate(classes, axis=0), tables)
@@ -599,8 +600,8 @@
     own_copies[0].start()
     for s in range(4):
         bulk_stage(parity, s)
-    for n, copy in enumerate(face_copies()):
-        pl.when(exists[n ^ 1])(copy.wait_recv)
+    for n, copy in enumerate(face_copies(0) + face_copies(1)):
+        pl.when(exists[n % 4 ^ 1])(copy.wait_recv)
     for n, copy in enumerate(corner_copies()):
         pl.when(exists[n ^ 1])(copy.wait_recv)
     gather_outer()
@@ -610,8 +611,8 @@
     own_copies[1].start()
     bulk_weave(parity)
     own_copies[2].start()
-    for n, copy in enumerate(face_copies()):
-        pl.when(exists[n])(copy.wait_send)
+    for n, copy in enumerate(face_copies(0) + face_copies(1)):
+        pl.when(exists[n % 4])(copy.wait_send)
     for n, copy in enumerate(corner_copies()):
         pl.when(exists[n])(copy.wait_send)
     land_copy.wait_send()
@@ -754,7 +755,8 @@
             strip_buf,
             pltpu.VMEM((8, 8, SIDE), f32),
             pltpu.VMEM((8, 8, SIDE), f32),
-            pltpu.VMEM((8, 4, 16, HALF), f32),
+            pltpu.VMEM((8, 36, HALF), f32),
+            pltpu.VMEM((8, 24, HALF), f32),
             pltpu.VMEM((2 * REACH + 1, 8, HALF), f32),
             outer_buf,
             outer_buf,
@@ -770,8 +772,8 @@
             pltpu.SemaphoreType.DMA((4,)),
             pltpu.SemaphoreType.DMA((5,)),
             pltpu.SemaphoreType.DMA,
-            pltpu.SemaphoreType.DMA((4,)),
-            pltpu.SemaphoreType.DMA((4,)),
+            pltpu.SemaphoreType.DMA((2, 4)),
+            pltpu.SemaphoreType.DMA((2, 4)),
             pltpu.SemaphoreType.DMA((2 * REACH,)),
             pltpu.SemaphoreType.DMA((2 * REACH,)),
             pltpu.SemaphoreType.DMA((3,)),

time: 20.8 us -> 20.8 us (level)
  no operation moved by 1% of the time
where the time goes in v10:
time: 20.8 us; the launch traced here: 20.6 us
  Pallas kernels  20.6 us (99%)
    pallas_call x1, Pallas kernels, body(): pl.pallas_call(functools.partial(kernel, owners), out_shape=(results, rin...  17.4 us
    pallas_call x1, Pallas kernels, body(): pl.pallas_call(merge_kernel, out_shape=jax.ShapeDtypeStruct((3, 3, SIDE,...  3.21 us

profile of v10, /device:TPU:25, one launch (start us, length us, event | category | flops | bytes accessed | tf_op | source)
XLA Modules:
  0.0 20.6 jit_solution(1424819291157445480)
XLA Ops:
  0.0 17.4 %regrid_step.1 = (f32[3,3,2,256,128]{4,3,2,1,0:T(8,128)}, f32[3,3,4,8,256]{4,3,2,1,0:T(8,128)}) custom-call(s32[2]{0:T(128)} %parents_hbm.1, s32[128]{0:T(128)} %counts_hbm.3, s32[4,256]{1,0:T(4,128)} %bitcast.1, f32[11]{0:T(128)} %diff_hbm.1, f32[11]{0:T(128)} %grow_hbm.1, f32[1,3,256,256]{3,2,1,0:T(8,128)} %coarse_ref.1, s32[3,256,256]{2,1,0:T(8,128)} %land_ref.1), custom_call_target="tpu_custom_call" | custom-call | tf_op jit(solution)/shard_map/regrid_step/pallas_call | solution.py:731
  17.4 3.2 %merge_slots.1 = f32[3,3,256,256]{3,2,1,0:T(8,128)} custom-call(s32[128]{0:T(128)} %counts_hbm.3, f32[3,3,2,256,128]{4,3,2,1,0:T(8,128)} %get-tuple-element.7.result_hbm, f32[3,3,4,8,256]{4,3,2,1,0:T(8,128)} %get-tuple-element.8.ring_hbm), custom_call_target="tpu_custom_call" | custom-call | tf_op jit(solution)/shard_map/merge_slots/pallas_call | solution.py:788
